TPU v7x, 256 devices: a whole 4x4x8 slice. The times are simulated.
256 devices in a mesh: task: 32 (over z, x), tp: 8 (over y, core).
Axes of the slice: x: 4, y: 4, z: 8, core: 2. Of those that a mesh axis runs over, the one named last changes fastest.
Arguments:
- queries: bfloat16 [3072, 8192], P('task', 'tp'), may hold values from -110 to 110
- prompt_keys: bfloat16 [131072, 1024], P('task', 'tp'), may hold values from -6 to 6
- prompt_values: bfloat16 [131072, 1024], P('task', 'tp'), may hold values from -6 to 6
- suffix_keys: bfloat16 [262144, 1024], P('task', 'tp'), may hold values from -6 to 6
- suffix_values: bfloat16 [262144, 1024], P('task', 'tp'), may hold values from -6 to 6
- new_keys: bfloat16 [3072, 1024], P('task', 'tp'), may hold values from -6 to 6
- new_values: bfloat16 [3072, 1024], P('task', 'tp'), may hold values from -6 to 6
- out_weight: bfloat16 [8192, 8192], P('tp', 'task'), may hold values from -0.5 to 0.5
- span_perm: int32 [512], P('task'), may hold values from 0 to 511, each once
- share_counts: int32 [16], replicated, may hold values from 1 to 160, 1024 in all
- sample_perm: int32 [1024], replicated, may hold values from 0 to 1023, each once
- decoded_lens: int32 [1024], P('task'), may hold values from 1 to 256, as said below
Outputs:
- head_mix: float32 [3072, 8192], P('tp', 'task')
Inputs may be any that keep to these rules, and one draw needn't show every extreme that they name: `decoded_lens`: every sample has decoded at least one token; some sample has filled all 256 slots. `share_counts`: the counts sum to 1024; some prompt has exactly 160 samples. `span_perm`: every prompt block stands in exactly one task slot.
All inputs are finite; a program needn't handle non-finite values.
Results may differ from a plain program's by a relative error of at most 0.008.
Values may be sent and summed in bfloat16 or wider, within the bound.
A program may use at most 128 MiB of HBM per device.

v0:
```python
import math

import jax
import jax.numpy as jnp
from jax import lax
from jax.sharding import PartitionSpec as P

H = 64
KVH = 8
HD = 128
PLEN = 8192
SPAN = 256
MAXSHARE = 160
SUF = 256


lowest = -1e30


def on_device(
    queries,
    prompt_keys,
    prompt_values,
    suffix_keys,
    suffix_values,
    new_keys,
    new_values,
    out_weight,
    span_perm,
    share_counts,
    sample_perm,
    decoded_lens,
):
    grouped = H // KVH
    kv_local = prompt_keys.shape[1] // HD
    own_count = decoded_lens.shape[0]
    total_samples = sample_perm.shape[0]
    slot_count = span_perm.shape[0]
    scaling = 1.0 / math.sqrt(HD)
    rows_block = 64
    table_width = -(-MAXSHARE // rows_block) * rows_block
    prompt_ends = jnp.cumsum(share_counts)
    prompt_starts = prompt_ends - share_counts
    inverse = (
        jnp.zeros((total_samples,), jnp.int32)
        .at[sample_perm]
        .set(jnp.arange(total_samples, dtype=jnp.int32))
    )
    rank_list = jnp.arange(table_width, dtype=jnp.int32)
    places = jnp.clip(prompt_starts[:, None] + rank_list[None, :], 0, total_samples - 1)
    members = jnp.where(rank_list[None, :] < share_counts[:, None], inverse[places], total_samples)
    span_prompt = span_perm // (PLEN // SPAN)
    every_query = lax.all_gather(queries, "task", axis=0, tiled=True).reshape(
        total_samples, 3, kv_local, grouped, HD
    )
    key_slots = prompt_keys.reshape(slot_count, SPAN, kv_local, HD)
    value_slots = prompt_values.reshape(slot_count, SPAN, kv_local, HD)

    def block_scores(slot_index, first_member):
        prompt = span_prompt[slot_index]
        sample_ids = lax.dynamic_slice_in_dim(members[prompt], first_member, rows_block)
        picked = every_query[jnp.minimum(sample_ids, total_samples - 1)]
        scores = (
            jnp.einsum(
                "sjkgd,ckd->sjkgc",
                picked,
                key_slots[slot_index],
                preferred_element_type=jnp.float32,
            )
            * scaling
        )
        return (sample_ids, scores)

    def block_trips(slot_index):
        return (share_counts[span_prompt[slot_index]] + rows_block - 1) // rows_block

    own_query = queries.reshape(own_count, 3, kv_local, grouped, HD)
    suffix_scores = (
        jnp.einsum(
            "sjkgd,stkd->sjkgt",
            own_query,
            suffix_keys.reshape(own_count, SUF, kv_local, HD),
            preferred_element_type=jnp.float32,
        )
        * scaling
    )
    fresh_scores = (
        jnp.einsum(
            "sjkgd,stkd->sjkgt",
            own_query,
            new_keys.reshape(own_count, 3, kv_local, HD),
            preferred_element_type=jnp.float32,
        )
        * scaling
    )
    suffix_valid = (jnp.arange(SUF)[None, :] < decoded_lens[:, None])[:, None, None, None, :]
    fresh_valid = (jnp.arange(3)[None, :] <= jnp.arange(3)[:, None])[None, :, None, None, :]
    own_max = jnp.maximum(
        jnp.max(jnp.where(suffix_valid, suffix_scores, lowest), axis=-1),
        jnp.max(jnp.where(fresh_valid, fresh_scores, lowest), axis=-1),
    )
    zero_totals = jnp.zeros((total_samples, 3, kv_local, grouped), jnp.float32)
    zero_outputs = jnp.zeros((total_samples, 3, kv_local, grouped, HD), jnp.float32)

    def max_slot(slot_index, maxima):

        def max_block(block_step, running):
            sample_ids, scores = block_scores(slot_index, block_step * rows_block)
            return running.at[sample_ids].max(jnp.max(scores, axis=-1), mode="drop")

        return lax.fori_loop(0, block_trips(slot_index), max_block, maxima)

    maxima = jnp.full((total_samples, 3, kv_local, grouped), lowest, jnp.float32)
    maxima = lax.fori_loop(0, slot_count, max_slot, maxima)
    offset = lax.axis_index("task") * own_count
    own_rows = lax.dynamic_slice_in_dim(maxima, offset, own_count)
    maxima = lax.dynamic_update_slice_in_dim(maxima, jnp.maximum(own_rows, own_max), offset, 0)
    maxima = lax.pmax(maxima, "task")

    def sum_slot(slot_index, running):

        def sum_block(block_step, inner):
            totals, outputs = inner
            sample_ids, scores = block_scores(slot_index, block_step * rows_block)
            row_tops = maxima[jnp.minimum(sample_ids, total_samples - 1)]
            weights = jnp.exp(scores - row_tops[..., None]).astype(jnp.bfloat16)
            totals = totals.at[sample_ids].add(
                jnp.sum(weights, axis=-1, dtype=jnp.float32), mode="drop"
            )
            products = jnp.einsum(
                "sjkgc,ckd->sjkgd",
                weights,
                value_slots[slot_index],
                preferred_element_type=jnp.float32,
            )
            outputs = outputs.at[sample_ids].add(products, mode="drop")
            return (totals, outputs)

        return lax.fori_loop(0, block_trips(slot_index), sum_block, running)

    totals, outputs = lax.fori_loop(0, slot_count, sum_slot, (zero_totals, zero_outputs))
    totals, outputs = (
        lax.psum_scatter(totals, "task", scatter_dimension=0, tiled=True),
        lax.psum_scatter(outputs, "task", scatter_dimension=0, tiled=True),
    )
    row_top = lax.dynamic_slice_in_dim(maxima, offset, own_count)
    suffix_weights = jnp.where(
        suffix_valid, jnp.exp(suffix_scores - row_top[..., None]), 0.0
    ).astype(jnp.bfloat16)
    fresh_weights = jnp.where(fresh_valid, jnp.exp(fresh_scores - row_top[..., None]), 0.0).astype(
        jnp.bfloat16
    )
    extra_total = jnp.sum(suffix_weights, axis=-1, dtype=jnp.float32) + jnp.sum(
        fresh_weights, axis=-1, dtype=jnp.float32
    )
    extra_output = jnp.einsum(
        "sjkgt,stkd->sjkgd",
        suffix_weights,
        suffix_values.reshape(own_count, SUF, kv_local, HD),
        preferred_element_type=jnp.float32,
    )
    extra_output = extra_output + jnp.einsum(
        "sjkgt,stkd->sjkgd",
        fresh_weights,
        new_values.reshape(own_count, 3, kv_local, HD),
        preferred_element_type=jnp.float32,
    )
    extra_total, extra_output = (extra_total, extra_output)
    totals = totals + extra_total
    outputs = outputs + extra_output
    attended = (
        (outputs / totals[..., None])
        .astype(jnp.bfloat16)
        .reshape(own_count * 3, kv_local * grouped * HD)
    )
    every_row = lax.all_gather(attended, "task", axis=0, tiled=True)
    return lax.psum_scatter(
        jnp.dot(every_row, out_weight, preferred_element_type=jnp.float32),
        "tp",
        scatter_dimension=0,
        tiled=True,
    )


def solution(mesh):
    return jax.shard_map(
        on_device,
        mesh=mesh,
        in_specs=(
            P("task", "tp"),
            P("task", "tp"),
            P("task", "tp"),
            P("task", "tp"),
            P("task", "tp"),
            P("task", "tp"),
            P("task", "tp"),
            P("tp", "task"),
            P("task"),
            P(),
            P(),
            P("task"),
        ),
        out_specs=P("tp", "task"),
        check_vma=False,
    )
```

profile of v0, /device:TPU:49, one launch (start us, length us, event | category | flops | bytes accessed | tf_op | source)
XLA Modules:
  0.0 1929.5 jit_solution(15912969226863478691)
XLA Ops:
  30.1 68.9 %all-gather.3.cloned.1.call-done = bf16[3072,1024]{1,0:T(8,128)(2,1)} async-done(((bf16[96,1024]{1,0:T(8,128)(2,1)}), bf16[3072,1024]{1,0:T(8,128)(2,1)}) %all-gather.3.cloned.1.call-update) | async-done | bytes 6291472 | tf_op jit(solution)/shard_map/all_gather | solution.py:53
  107.6 343.0 %while.101 = (s32[]{:T(128)}, f32[1024,3,1,8]{3,1,0,2:T(4,128)}, s32[16]{0:T(128)S(1)}, s32[16]{0:T(128)S(1)}, bf16[16,256,1,128]{3,1,2,0:T(8,128)(2,1)}, /*inde...) while((s32[]{:T(128)}, f32[1024,3,1,8]{3,1,0,2:T(4,128)}, ...), condition=%wide.region_7.8_spmd, body=%wide.region_2.7_spmd.sunk | while | flops 101451232 | bytes 1407184 | solution.py:114
  127.5 32.2 %while.104 = (s32[]{:T(128)}, f32[1024,3,1,8]{3,1,0,2:T(4,128)}, s32[]{:T(128)}, s32[16,192]{1,0:T(8,128)S(1)}, s32[]{:T(128)}, /*index=5*/bf16[1024,3,1,8,128]{...) while((s32[]{:T(128)}, f32[1024,3,1,8]{3,1,0,2:T(4,128)}, ...), condition=%wide.region_6.6_spmd, body=%wide.region_3.5_spmd.sunk | while | flops 101451208 | bytes 1275579 | solution.py:111
  164.3 32.2 %while.104 = (s32[]{:T(128)}, f32[1024,3,1,8]{3,1,0,2:T(4,128)}, s32[]{:T(128)}, s32[16,192]{1,0:T(8,128)S(1)}, s32[]{:T(128)}, /*index=5*/bf16[1024,3,1,8,128]{...) while((s32[]{:T(128)}, f32[1024,3,1,8]{3,1,0,2:T(4,128)}, ...), condition=%wide.region_6.6_spmd, body=%wide.region_3.5_spmd.sunk | while | flops 101451208 | bytes 1275579 | solution.py:111
  262.7 21.5 %while.104 = (s32[]{:T(128)}, f32[1024,3,1,8]{3,1,0,2:T(4,128)}, s32[]{:T(128)}, s32[16,192]{1,0:T(8,128)S(1)}, s32[]{:T(128)}, /*index=5*/bf16[1024,3,1,8,128]{...) while((s32[]{:T(128)}, f32[1024,3,1,8]{3,1,0,2:T(4,128)}, ...), condition=%wide.region_6.6_spmd, body=%wide.region_3.5_spmd.sunk | while | flops 101451208 | bytes 1275579 | solution.py:111
  350.5 32.2 %while.104 = (s32[]{:T(128)}, f32[1024,3,1,8]{3,1,0,2:T(4,128)}, s32[]{:T(128)}, s32[16,192]{1,0:T(8,128)S(1)}, s32[]{:T(128)}, /*index=5*/bf16[1024,3,1,8,128]{...) while((s32[]{:T(128)}, f32[1024,3,1,8]{3,1,0,2:T(4,128)}, ...), condition=%wide.region_6.6_spmd, body=%wide.region_3.5_spmd.sunk | while | flops 101451208 | bytes 1275579 | solution.py:111
  418.2 32.4 %while.104 = (s32[]{:T(128)}, f32[1024,3,1,8]{3,1,0,2:T(4,128)}, s32[]{:T(128)}, s32[16,192]{1,0:T(8,128)S(1)}, s32[]{:T(128)}, /*index=5*/bf16[1024,3,1,8,128]{...) while((s32[]{:T(128)}, f32[1024,3,1,8]{3,1,0,2:T(4,128)}, ...), condition=%wide.region_6.6_spmd, body=%wide.region_3.5_spmd.sunk | while | flops 101451208 | bytes 1275579 | solution.py:111
  454.5 197.7 %all-reduce.4.cloned.1.call-done = f32[1024,3,1,8]{0,3,2,1:T(8,128)} async-done(((f32[1024,3,1,8]{0,3,2,1:T(8,128)}), f32[1024,3,1,8]{0,3,2,1:T(8,128)}) %all-reduce.4.cloned.1.call-update) | async-done | bytes 98320 | tf_op jit(solution)/shard_map/pmax | solution.py:118
  661.6 609.2 %while.103 = (s32[]{:T(128)}, f32[1024,3,1,8]{3,1,0,2:T(4,128)}, f32[1024,3,1,8,128]{4,3,1,0,2:T(8,128)}, s32[16]{0:T(128)S(1)}, s32[16]{0:T(128)S(1)}, /*index=...) while((s32[]{:T(128)}, f32[1024,3,1,8]{3,1,0,2:T(4,128)}, ...), condition=%wide.region_17.18_spmd, body=%wide.region_11.17_spmd.sunk | while | flops 203490768 | bytes 6341400 | solution.py:141
  692.4 64.0 %while.105 = (s32[]{:T(128)}, f32[1024,3,1,8]{3,1,0,2:T(4,128)}, f32[1024,3,1,8,128]{4,3,1,0,2:T(8,128)}, s32[]{:T(128)}, s32[16,192]{1,0:T(8,128)S(1)}, /*index...) while((s32[]{:T(128)}, f32[1024,3,1,8]{3,1,0,2:T(4,128)}, ...), condition=%wide.region_16.16_spmd, body=%wide.region_12.15_spmd.sunk | while | flops 203490752 | bytes 6078675 | solution.py:139
  761.1 64.0 %while.105 = (s32[]{:T(128)}, f32[1024,3,1,8]{3,1,0,2:T(4,128)}, f32[1024,3,1,8,128]{4,3,1,0,2:T(8,128)}, s32[]{:T(128)}, s32[16,192]{1,0:T(8,128)S(1)}, /*index...) while((s32[]{:T(128)}, f32[1024,3,1,8]{3,1,0,2:T(4,128)}, ...), condition=%wide.region_16.16_spmd, body=%wide.region_12.15_spmd.sunk | while | flops 203490752 | bytes 6078675 | solution.py:139
  829.9 21.3 %while.105 = (s32[]{:T(128)}, f32[1024,3,1,8]{3,1,0,2:T(4,128)}, f32[1024,3,1,8,128]{4,3,1,0,2:T(8,128)}, s32[]{:T(128)}, s32[16,192]{1,0:T(8,128)S(1)}, /*index...) while((s32[]{:T(128)}, f32[1024,3,1,8]{3,1,0,2:T(4,128)}, ...), condition=%wide.region_16.16_spmd, body=%wide.region_12.15_spmd.sunk | while | flops 203490752 | bytes 6078675 | solution.py:139
  907.8 21.5 %while.105 = (s32[]{:T(128)}, f32[1024,3,1,8]{3,1,0,2:T(4,128)}, f32[1024,3,1,8,128]{4,3,1,0,2:T(8,128)}, s32[]{:T(128)}, s32[16,192]{1,0:T(8,128)S(1)}, /*index...) while((s32[]{:T(128)}, f32[1024,3,1,8]{3,1,0,2:T(4,128)}, ...), condition=%wide.region_16.16_spmd, body=%wide.region_12.15_spmd.sunk | while | flops 203490752 | bytes 6078675 | solution.py:139
  934.1 42.7 %while.105 = (s32[]{:T(128)}, f32[1024,3,1,8]{3,1,0,2:T(4,128)}, f32[1024,3,1,8,128]{4,3,1,0,2:T(8,128)}, s32[]{:T(128)}, s32[16,192]{1,0:T(8,128)S(1)}, /*index...) while((s32[]{:T(128)}, f32[1024,3,1,8]{3,1,0,2:T(4,128)}, ...), condition=%wide.region_16.16_spmd, body=%wide.region_12.15_spmd.sunk | while | flops 203490752 | bytes 6078675 | solution.py:139
  1033.6 21.5 %while.105 = (s32[]{:T(128)}, f32[1024,3,1,8]{3,1,0,2:T(4,128)}, f32[1024,3,1,8,128]{4,3,1,0,2:T(8,128)}, s32[]{:T(128)}, s32[16,192]{1,0:T(8,128)S(1)}, /*index...) while((s32[]{:T(128)}, f32[1024,3,1,8]{3,1,0,2:T(4,128)}, ...), condition=%wide.region_16.16_spmd, body=%wide.region_12.15_spmd.sunk | while | flops 203490752 | bytes 6078675 | solution.py:139
  1059.9 21.2 %while.105 = (s32[]{:T(128)}, f32[1024,3,1,8]{3,1,0,2:T(4,128)}, f32[1024,3,1,8,128]{4,3,1,0,2:T(8,128)}, s32[]{:T(128)}, s32[16,192]{1,0:T(8,128)S(1)}, /*index...) while((s32[]{:T(128)}, f32[1024,3,1,8]{3,1,0,2:T(4,128)}, ...), condition=%wide.region_16.16_spmd, body=%wide.region_12.15_spmd.sunk | while | flops 203490752 | bytes 6078675 | solution.py:139
  1085.9 64.0 %while.105 = (s32[]{:T(128)}, f32[1024,3,1,8]{3,1,0,2:T(4,128)}, f32[1024,3,1,8,128]{4,3,1,0,2:T(8,128)}, s32[]{:T(128)}, s32[16,192]{1,0:T(8,128)S(1)}, /*index...) while((s32[]{:T(128)}, f32[1024,3,1,8]{3,1,0,2:T(4,128)}, ...), condition=%wide.region_16.16_spmd, body=%wide.region_12.15_spmd.sunk | while | flops 203490752 | bytes 6078675 | solution.py:139
  1154.6 21.3 %while.105 = (s32[]{:T(128)}, f32[1024,3,1,8]{3,1,0,2:T(4,128)}, f32[1024,3,1,8,128]{4,3,1,0,2:T(8,128)}, s32[]{:T(128)}, s32[16,192]{1,0:T(8,128)S(1)}, /*index...) while((s32[]{:T(128)}, f32[1024,3,1,8]{3,1,0,2:T(4,128)}, ...), condition=%wide.region_16.16_spmd, body=%wide.region_12.15_spmd.sunk | while | flops 203490752 | bytes 6078675 | solution.py:139
  1180.8 21.3 %while.105 = (s32[]{:T(128)}, f32[1024,3,1,8]{3,1,0,2:T(4,128)}, f32[1024,3,1,8,128]{4,3,1,0,2:T(8,128)}, s32[]{:T(128)}, s32[16,192]{1,0:T(8,128)S(1)}, /*index...) while((s32[]{:T(128)}, f32[1024,3,1,8]{3,1,0,2:T(4,128)}, ...), condition=%wide.region_16.16_spmd, body=%wide.region_12.15_spmd.sunk | while | flops 203490752 | bytes 6078675 | solution.py:139
  1206.8 64.0 %while.105 = (s32[]{:T(128)}, f32[1024,3,1,8]{3,1,0,2:T(4,128)}, f32[1024,3,1,8,128]{4,3,1,0,2:T(8,128)}, s32[]{:T(128)}, s32[16,192]{1,0:T(8,128)S(1)}, /*index...) while((s32[]{:T(128)}, f32[1024,3,1,8]{3,1,0,2:T(4,128)}, ...), condition=%wide.region_16.16_spmd, body=%wide.region_12.15_spmd.sunk | while | flops 203490752 | bytes 6078675 | solution.py:139
  1281.7 269.8 %all-reduce.6.cloned.1.call-done = f32[1024,3,1,8]{3,2,1,0:T(1,128)} async-done(((f32[1024,3,1,8]{3,2,1,0:T(1,128)}), f32[1024,3,1,8]{3,2,1,0:T(1,128)}) %all-reduce.6.cloned.1.call-update) | async-done | bytes 98320
  1552.6 237.8 %reduce-scatter.3.cloned.1.call-done = f32[32,3,1,8,128]{4,3,1,0,2:T(8,128)} async-done(((f32[1024,3,1,8,128]{4,3,1,0,2:T(8,128)}), f32[32,3,1,8,128]{4,3,1,0,2:T(8,128)}) %reduce-scatter.3.cloned.1.call-update) | async-done | bytes 393232 | tf_op jit(solution)/shard_map/reduce_scatter | solution.py:144
  1792.8 89.9 %all-gather.5.cloned.1.call-done = bf16[3072,1024]{1,0:T(8,128)(2,1)} async-done(((bf16[96,1024]{1,0:T(8,128)(2,1)}), bf16[3072,1024]{1,0:T(8,128)(2,1)}) %all-gather.5.cloned.1.call-update) | async-done | bytes 6291472 | tf_op jit(solution)/shard_map/all_gather | solution.py:176
  1889.0 33.7 %reduce-scatter.5.cloned.1.call-done = f32[384,256]{1,0:T(8,128)} async-done(((f32[3072,256]{1,0:T(8,128)}), f32[384,256]{1,0:T(8,128)}) %reduce-scatter.5.cloned.1.call-update) | async-done | bytes 393232 | tf_op jit(solution)/shard_map/reduce_scatter | solution.py:177
  (527 shorter events, 1157.5 us)
Async XLA Ops:
  6.5 22.0 %copy-start = (bf16[8192,128]{1,0:T(8,128)(2,1)S(1)}, bf16[8192,128]{1,0:T(8,128)(2,1)}, u32[]{:S(2)}) copy-start(bf16[8192,128]{1,0:T(8,128)(2,1)} %param.23) | copy-start | bytes 6291460
  6.5 92.5 %all-gather.3.cloned.1.call-start = ((), (), s32[]{:S(2)}) async-start(), calls=%async_computation.2 | async-start | bytes 6488064 | tf_op jit(solution)/shard_map/all_gather | solution.py:53
  7.3 644.9 %all-reduce.4.cloned.1.call-start = ((), (), s32[]{:S(2)}) async-start(), calls=%async_computation.3 | async-start | bytes 196608 | tf_op jit(solution)/shard_map/pmax | solution.py:118
  14.0 12.8 copy-start.7
  14.0 12.8 copy-start.2
  14.1 14.3 copy-start.14
  14.1 14.3 copy-start.12
  14.1 14.4 copy-start.9
  26.9 79.1 %copy-start.10 = (pred[3,3]{1,0:T(4,128)(4,1)}, pred[3,3]{1,0:T(4,128)(4,1)S(1)}, u32[]{:S(2)}) copy-start(pred[3,3]{1,0:T(4,128)(4,1)S(1)} %iota_compare_fusion.2) | copy-start | bytes 31
  28.4 77.6 %copy-start.5 = (pred[32,256]{1,0:T(8,128)(4,1)}, pred[32,256]{1,0:T(8,128)(4,1)S(1)}, u32[]{:S(2)}) copy-start(pred[32,256]{1,0:T(8,128)(4,1)S(1)} %iota_compare_fusion) | copy-start | bytes 24580
  453.6 0.6 copy-start.3
  454.3 1097.3 %all-reduce.6.cloned.1.call-start = ((), (), s32[]{:S(2)}) async-start(), calls=%async_computation.7 | async-start | bytes 3145728
  1275.3 515.1 %reduce-scatter.3.cloned.1.call-start = ((), (), s32[]{:S(2)}) async-start(), calls=%async_computation.4 | async-start | bytes 12976128 | tf_op jit(solution)/shard_map/reduce_scatter | solution.py:144
  1275.3 0.7 copy-start.8
  1275.3 0.8 copy-start.15
  1275.3 2.9 copy-start.4
  1275.3 2.9 copy-start.11
  1275.3 3.1 copy-start.1
  1275.4 3.1 copy-start.6
  1275.8 606.8 %all-gather.5.cloned.1.call-start = ((), (), s32[]{:S(2)}) async-start(), calls=%async_computation.5 | async-start | bytes 6488064 | tf_op jit(solution)/shard_map/all_gather | solution.py:176
  1281.7 600.9 %copy-start.13 = (bf16[1024,256]{1,0:T(8,128)(2,1)S(1)}, bf16[1024,256]{1,0:T(8,128)(2,1)}, u32[]{:S(2)}) copy-start(bf16[1024,256]{1,0:T(8,128)(2,1)} %param.27) | copy-start | bytes 1572868
  1792.7 129.9 %reduce-scatter.5.cloned.1.call-start = ((), (), s32[]{:S(2)}) async-start(), calls=%async_computation.6 | async-start | bytes 3538944 | tf_op jit(solution)/shard_map/reduce_scatter | solution.py:177
Sparse Core Ops, SparseCore 0:
  9.9 89.0 all-gather.2
  454.4 197.7 all-reduce.3
  1275.4 276.1 all-reduce.5
  1555.6 234.7 reduce-scatter.2
  1792.8 89.8 all-gather.4
  1889.1 33.4 reduce-scatter.4
where the time goes:
time: 1960 us; the launch traced here: 1930 us
  waiting for transfers between devices  899 us (46%)
  other arithmetic  536 us (27%)
  local copies, waits for them, and re-layouts  341 us (17%)
  loops' own time  84.6 us (4%)
  matrix products  53.4 us (3%)
    unnamed x7, waiting for transfers between devices  271 us
    reduce_scatter x1, waiting for transfers between devices, on_device(): lax.psum_scatter(outputs, 'task', scatter_dimension=0, tiled=True)  238 us
    pmax x1, waiting for transfers between devices, on_device(): maxima = lax.pmax(maxima, 'task')  198 us
    scatter-add x25, other arithmetic, sum_block(): outputs = outputs.at[sample_ids].add(products, mode='drop')  192 us
    gather x50, local copies, waits for them, and re-layouts, block_scores(): picked = every_query[jnp.minimum(sample_ids, total_samples - 1)]  172 us
    another operation x25, other arithmetic, max_block(): return running.at[sample_ids].max(jnp.max(scores, axis=-1), mode='drop')  168 us
    scatter-add x25, other arithmetic, sum_block(): totals.at[sample_ids]  168 us
    all_gather x1, waiting for transfers between devices, on_device(): every_row = lax.all_gather(attended, 'task', axis=0, tiled=True)  89.9 us
  transfers between devices with their start and end apart: 6, of which 6 were waited for; matrix products, arithmetic and copies ran while one was open for 1% of the time, Pallas kernels for 0%

commit v1 on v0

v1 whole, which is shorter than its diff:
```python
import functools
import math

import jax
import jax.numpy as jnp
from jax import lax
from jax.experimental import pallas as pl
from jax.experimental.pallas import tpu as pltpu
from jax.sharding import PartitionSpec as P

H = 64
KVH = 8
HD = 128
PLEN = 8192
SPAN = 256
SUF = 256
NZ = 8
NX = 4
TASKS = NZ * NX
SHARD = 768
OWN = 32
CHUNK = 16
ROWS = CHUNK * 24
SLOTS = 16
GROUPS = SHARD // 128
LOWEST = -1.0e30
MESH_ID = pl.DeviceIdType.MESH
F32 = jnp.float32
BF16 = jnp.bfloat16
LOG2E = math.log2(math.e)
SCALE = 1.0 / math.sqrt(HD)
XROWS = 256


class Hop:
    def __init__(self, index, axis, way, dz, dx, low, high, deps):
        self.index, self.axis, self.way = index, axis, way
        self.dz, self.dx, self.low, self.high, self.deps = dz, dx, low, high, deps
        self.kids = []


def gather_tree():
    hops = []

    def add(axis, way, dz, dx, rows, deps):
        hop = Hop(len(hops), axis, way, dz, dx, rows[0], rows[1], deps)
        hops.append(hop)
        return hop

    def ring(axis, size, rows, base, dz, dx):
        middle = (rows[0] + rows[1]) // 2
        held = {0: base}
        far = size // 2
        for way in (1, -1):
            deps = base
            for step in range(1, far):
                place = (step * way, dx) if axis == "z" else (dz, step * way)
                deps = [add(axis, way, place[0], place[1], rows, deps)]
                held[step * way] = deps
            half = (rows[0], middle) if way == 1 else (middle, rows[1])
            place = (far, dx) if axis == "z" else (dz, far)
            held.setdefault(far, []).append(add(axis, way, place[0], place[1], half, deps))
        return held

    rows_x, rows_z = (0, XROWS), (XROWS, SHARD)
    for dx, base in ring("x", NX, rows_x, [], 0, 0).items():
        ring("z", NZ, rows_x, base, 0, dx)
    for dz, base in ring("z", NZ, rows_z, [], 0, 0).items():
        ring("x", NX, rows_z, base, dz, 0)
    for hop in hops:
        for dep in hop.deps:
            dep.kids.append(hop)
    free, arrival = {}, {}
    pending = [(0.0, hop.index) for hop in hops if not hop.deps]
    while pending:
        pending.sort()
        ready, index = pending.pop(0)
        hop = hops[index]
        link = (hop.axis, hop.way)
        start = max(ready, free.get(link, 0.0))
        free[link] = start + (hop.high - hop.low) * 256 * 2 / 90e3
        arrival[index] = free[link] + 1.0
        for kid in hop.kids:
            if all(dep.index in arrival for dep in kid.deps):
                pending.append((max(arrival[dep.index] for dep in kid.deps), kid.index))
    return sorted(hops, key=lambda hop: arrival[hop.index])


TREE = gather_tree()


def place():
    task = lax.axis_index("task")
    return task // NX, lax.rem(task, NX)


def task_at(z, x):
    return lax.rem(z + 2 * NZ, NZ) * NX + lax.rem(x + 2 * NX, NX)


def greet_neighbours(z, x):
    barrier = pltpu.get_barrier_semaphore()
    for dz, dx in ((1, 0), (-1, 0), (0, 1), (0, -1)):
        pl.semaphore_signal(
            barrier, inc=1, device_id={"task": task_at(z + dz, x + dx)}, device_id_type=MESH_ID
        )
    pl.semaphore_wait(barrier, 4)


def suffix_pair(pair, q_ref, sk_ref, sv_ref, nk_ref, nv_ref, lens_ref, o_ref, lam_ref):
    q = q_ref[pl.ds(48 * pair, 48), :]
    row = lax.broadcasted_iota(jnp.int32, (48, SUF), 0)
    col = lax.broadcasted_iota(jnp.int32, (48, SUF), 1)
    first = row < 24
    nt = (((1,), (1,)), ((), ()))
    k0 = sk_ref[pl.ds(512 * pair, SUF), :]
    k1 = sk_ref[pl.ds(512 * pair + SUF, SUF), :]
    s0 = lax.dot_general(q, k0, nt, preferred_element_type=F32)
    s1 = lax.dot_general(q, k1, nt, preferred_element_type=F32)
    length = jnp.where(first, lens_ref[2 * pair], lens_ref[2 * pair + 1])
    s = jnp.where(col < length, jnp.where(first, s0, s1) * SCALE, LOWEST)
    f = lax.dot_general(q, nk_ref[...], nt, preferred_element_type=F32) * SCALE
    frow = lax.broadcasted_iota(jnp.int32, (48, 96), 0)
    fcol = lax.broadcasted_iota(jnp.int32, (48, 96), 1)
    later = jnp.where(frow < 24, 0, 1)
    position = (frow - 24 * later) >> 3
    ahead = fcol - 3 * (2 * pair + later)
    f = jnp.where((ahead >= 0) & (ahead <= position), f, LOWEST)
    top = jnp.maximum(jnp.max(s, axis=-1, keepdims=True), jnp.max(f, axis=-1, keepdims=True))
    ws = jnp.exp(s - top)
    wf = jnp.exp(f - top).astype(BF16)
    w0 = jnp.where(first, ws, 0.0).astype(BF16)
    w1 = jnp.where(first, 0.0, ws).astype(BF16)
    total = jnp.sum(w0.astype(F32) + w1.astype(F32), axis=-1, keepdims=True) + jnp.sum(
        wf.astype(F32), axis=-1, keepdims=True
    )
    out = jnp.dot(w0, sv_ref[pl.ds(512 * pair, SUF), :], preferred_element_type=F32)
    out = out + jnp.dot(w1, sv_ref[pl.ds(512 * pair + SUF, SUF), :], preferred_element_type=F32)
    out = out + jnp.dot(wf, nv_ref[...], preferred_element_type=F32)
    o_ref[pl.ds(48 * pair, 48), :] = out / total
    lam_ref[pl.ds(48 * pair, 48), :] = jnp.broadcast_to(top + jnp.log(total), (48, 128))


def gather_kernel(
    q_ref, sk_ref, sv_ref, nk_ref, nv_ref, lens_ref, all_ref, o_ref, lam_ref,
    wide_ref, own_sem, send_sems, recv_sems,
):
    z, x = place()
    greet_neighbours(z, x)
    own = pltpu.make_async_copy(q_ref, all_ref.at[task_at(z, x)], own_sem)
    own.start()

    def copy(hop):
        sz, sx = (hop.way, 0) if hop.axis == "z" else (0, hop.way)
        origin = task_at(z - hop.dz + sz, x - hop.dx + sx)
        rows = pl.ds(hop.low, hop.high - hop.low)
        target = all_ref.at[origin, rows]
        return pltpu.make_async_remote_copy(
            src_ref=q_ref.at[rows] if not hop.deps else target,
            dst_ref=target,
            send_sem=send_sems.at[hop.index],
            recv_sem=recv_sems.at[hop.index],
            device_id={"task": task_at(z + sz, x + sx)},
            device_id_type=MESH_ID,
        )

    for hop in TREE:
        if not hop.deps:
            copy(hop).start()
    done = set()
    pair = 0
    for count, hop in enumerate(TREE):
        if count % 4 == 0 and pair < OWN // 2:
            suffix_pair(pair, q_ref, sk_ref, sv_ref, nk_ref, nv_ref, lens_ref, o_ref, wide_ref)
            pair += 1
        copy(hop).wait_recv()
        done.add(hop.index)
        for kid in hop.kids:
            if all(dep.index in done for dep in kid.deps):
                copy(kid).start()
    for g in range(GROUPS):
        lam_ref[g] = jnp.transpose(wide_ref[pl.ds(128 * g, 128), :])[0:1, :]
    own.wait()
    for hop in TREE:
        copy(hop).wait_send()


VMEM_SPEC = pl.BlockSpec(memory_space=pltpu.VMEM)
SMEM_SPEC = pl.BlockSpec(memory_space=pltpu.SMEM)
ANY_SPEC = pl.BlockSpec(memory_space=pl.ANY)


def gather_queries(q, suffix_keys, suffix_values, new_keys, new_values, lens):
    hops = len(TREE)
    return pl.pallas_call(
        gather_kernel,
        out_shape=(
            jax.ShapeDtypeStruct((TASKS, SHARD, HD), BF16),
            jax.ShapeDtypeStruct((SHARD, HD), F32),
            jax.ShapeDtypeStruct((GROUPS, 1, 128), F32),
        ),
        in_specs=[VMEM_SPEC] * 5 + [SMEM_SPEC],
        out_specs=(ANY_SPEC, VMEM_SPEC, VMEM_SPEC),
        scratch_shapes=[
            pltpu.VMEM((SHARD, 128), F32),
            pltpu.SemaphoreType.DMA,
            pltpu.SemaphoreType.DMA((hops,)),
            pltpu.SemaphoreType.DMA((hops,)),
        ],
        compiler_params=pltpu.CompilerParams(
            collective_id=0, has_side_effects=True, vmem_limit_bytes=48 * 2**20
        ),
        name="gather_queries",
    )(q, suffix_keys, suffix_values, new_keys, new_values, lens)


def prompt_kernel(
    order_ref, counts_ref, span_ref, q_ref, k_ref, v_ref, out_ref, lam_ref,
    o_ref, wide_ref, qs_ref, acc_ref, top_ref, blocks_ref, have_ref,
):
    for p in range(16):
        have_ref[p] = 0
    for slot in range(SLOTS):
        p = span_ref[slot] >> 5
        blocks_ref[p * SLOTS + have_ref[p]] = slot
        have_ref[p] = have_ref[p] + 1

    ones = jnp.ones((SPAN, 128), BF16)
    nt = (((1,), (1,)), ((), ()))

    def fill(first, count):
        def one(i, carry):
            at = pl.multiple_of(order_ref[first + i] * 24, 8)
            o_ref[pl.ds(at, 24), :] = jnp.zeros((24, 128), F32)
            wide_ref[pl.ds(at, 24), :] = jnp.full((24, 128), LOWEST, F32)
            return carry

        lax.fori_loop(0, count, one, 0)

    def attend(p, first, count):
        have = have_ref[p]

        def chunk(c, carry):
            base = first + c * CHUNK
            samples = [order_ref[jnp.minimum(base + i, first + count - 1)] for i in range(CHUNK)]
            for i, s in enumerate(samples):
                at = pl.multiple_of((s >> 1) * 48, 16)
                both = q_ref[pl.ds(at, 48), :].astype(F32)
                qs_ref[pl.ds(24 * i, 24), :] = jnp.where((s & 1) == 1, both[24:48], both[0:24])
            top_ref[...] = jnp.full((ROWS, 128), LOWEST, F32)
            acc_ref[...] = jnp.zeros((ROWS, 256), F32)

            def block(b, inner):
                slot = blocks_ref[p * SLOTS + b]
                at = pl.multiple_of(slot * SPAN, SPAN)
                keys = k_ref[pl.ds(at, SPAN), :]
                values = jnp.concatenate([v_ref[pl.ds(at, SPAN), :], ones], axis=1)
                for part in range(3):
                    rows = pl.ds(128 * part, 128)
                    q = qs_ref[rows, :].astype(BF16)
                    s = lax.dot_general(q, keys, nt, preferred_element_type=F32) * (SCALE * LOG2E)
                    old = top_ref[rows, :]
                    new = jnp.maximum(old, jnp.max(s, axis=-1, keepdims=True))
                    w = jnp.exp2(s - jnp.concatenate([new, new], axis=1)).astype(BF16)
                    decay = jnp.exp2(old - new)
                    acc_ref[rows, :] = acc_ref[rows, :] * jnp.concatenate(
                        [decay, decay], axis=1
                    ) + jnp.dot(w, values, preferred_element_type=F32)
                    top_ref[rows, :] = new
                return inner

            lax.fori_loop(0, have, block, 0)
            for i, s in enumerate(samples):
                rows = pl.ds(24 * i, 24)
                total = acc_ref[rows, pl.ds(128, 128)]
                at = pl.multiple_of(s * 24, 8)
                o_ref[pl.ds(at, 24), :] = acc_ref[rows, pl.ds(0, 128)] / total
                wide_ref[pl.ds(at, 24), :] = top_ref[rows, :] * (1.0 / LOG2E) + jnp.log(total)
            return carry

        lax.fori_loop(0, (count + CHUNK - 1) // CHUNK, chunk, 0)

    def prompt(p, first):
        count = counts_ref[p]

        @pl.when(have_ref[p] == 0)
        def _():
            fill(first, count)

        @pl.when(have_ref[p] > 0)
        def _():
            attend(p, first, count)

        return first + count

    lax.fori_loop(0, 16, prompt, 0)

    def finish(t, carry):
        at = pl.multiple_of(t * SHARD, SHARD)
        out_ref[pl.ds(at, SHARD), :] = o_ref[pl.ds(at, SHARD), :].astype(BF16)
        eye = lax.broadcasted_iota(jnp.int32, (128, 128), 0) == lax.broadcasted_iota(
            jnp.int32, (128, 128), 1
        )
        for g in range(GROUPS):
            tile = wide_ref[pl.ds(pl.multiple_of(at + 128 * g, 128), 128), :]
            lam_ref[t * GROUPS + g] = jnp.sum(jnp.where(eye, tile, 0.0), axis=0, keepdims=True)
        return carry

    lax.fori_loop(0, TASKS, finish, 0)


def attend_prompts(order, counts, spans, q_all, keys, values):
    rows = TASKS * SHARD
    return pl.pallas_call(
        prompt_kernel,
        out_shape=(
            jax.ShapeDtypeStruct((rows, HD), BF16),
            jax.ShapeDtypeStruct((TASKS * GROUPS, 1, 128), F32),
        ),
        in_specs=[SMEM_SPEC] * 3 + [VMEM_SPEC] * 3,
        out_specs=(VMEM_SPEC, VMEM_SPEC),
        scratch_shapes=[
            pltpu.VMEM((rows, 128), F32),
            pltpu.VMEM((rows, 128), F32),
            pltpu.VMEM((ROWS, 128), F32),
            pltpu.VMEM((ROWS, 256), F32),
            pltpu.VMEM((ROWS, 128), F32),
            pltpu.SMEM((16 * SLOTS,), jnp.int32),
            pltpu.SMEM((16,), jnp.int32),
        ],
        compiler_params=pltpu.CompilerParams(vmem_limit_bytes=56 * 2**20),
        name="attend_prompts",
    )(order, counts, spans, q_all.reshape(rows, HD), keys, values)


def merge_kernel(
    part_in, lam_in, own_ref, own_lam_ref, out_ref,
    part_ref, lam_ref, land_ref, lland_ref, in_sem, send_sems, recv_sems, lsend_sems, lrecv_sems,
):
    z, x = place()
    load = pltpu.make_async_copy(part_in, part_ref, in_sem.at[0])
    lload = pltpu.make_async_copy(lam_in, lam_ref, in_sem.at[1])
    load.start()
    lload.start()
    greet_neighbours(z, x)
    load.wait()
    lload.wait()
    offsets, at = {}, 0
    for hop in TREE:
        offsets[hop.index] = at
        at += hop.high - hop.low

    def copies(hop):
        origin = task_at(z - hop.dz, x - hop.dx)
        sz, sx = (hop.way, 0) if hop.axis == "z" else (0, hop.way)
        target = {"task": task_at(z - sz, x - sx)}
        size = hop.high - hop.low
        wide = pltpu.make_async_remote_copy(
            src_ref=part_ref.at[origin, pl.ds(hop.low, size)],
            dst_ref=land_ref.at[pl.ds(offsets[hop.index], size)],
            send_sem=send_sems.at[hop.index],
            recv_sem=recv_sems.at[hop.index],
            device_id=target,
            device_id_type=MESH_ID,
        )
        thin = pltpu.make_async_remote_copy(
            src_ref=lam_ref.at[pl.ds(origin * GROUPS + hop.low // 128, size // 128)],
            dst_ref=lland_ref.at[pl.ds(offsets[hop.index] // 128, size // 128)],
            send_sem=lsend_sems.at[hop.index],
            recv_sem=lrecv_sems.at[hop.index],
            device_id=target,
            device_id_type=MESH_ID,
        )
        return thin, wide

    waited = set()

    def merge(origin, low, high, kids, last):
        for hop in kids:
            if hop.index not in waited:
                waited.add(hop.index)
                for copy in copies(hop):
                    copy.wait_recv()
        for g in range(low // 128, high // 128):
            here = [hop for hop in kids if hop.low <= 128 * g < hop.high]
            if not here and not last:
                continue
            lams = [lam_ref[origin * GROUPS + g]]
            parts = [part_ref[origin, pl.ds(128 * g, 128), :].astype(F32)]
            for hop in here:
                start = offsets[hop.index] + 128 * g - hop.low
                lams.append(lland_ref[start // 128])
                parts.append(land_ref[pl.ds(start, 128), :].astype(F32))
            if last:
                lams.append(own_lam_ref[g])
                parts.append(own_ref[pl.ds(128 * g, 128), :])
            top = functools.reduce(jnp.maximum, lams)
            shares = [jnp.exp(lam - top) for lam in lams]
            total = functools.reduce(jnp.add, shares)
            mixed = parts[0]
            for share, part in zip(shares[1:], parts[1:]):
                weight = jnp.transpose(jnp.broadcast_to(share / total, (128, 128)))
                mixed = mixed + weight * (part - parts[0])
            if last:
                out_ref[pl.ds(128 * g, 128), :] = mixed
            else:
                lam_ref[origin * GROUPS + g] = top + jnp.log(total)
                part_ref[origin, pl.ds(128 * g, 128), :] = mixed.astype(BF16)

    for hop in reversed(TREE):
        if hop.kids:
            merge(task_at(z - hop.dz, x - hop.dx), hop.low, hop.high, hop.kids, False)
        for copy in copies(hop):
            copy.start()
    merge(task_at(z, x), 0, SHARD, [hop for hop in TREE if not hop.deps], True)
    for hop in TREE:
        for copy in copies(hop):
            copy.wait_send()


def merge_parts(parts, lams, own, own_lam):
    hops = len(TREE)
    landed = sum(hop.high - hop.low for hop in TREE)
    return pl.pallas_call(
        merge_kernel,
        out_shape=jax.ShapeDtypeStruct((SHARD, HD), F32),
        in_specs=[ANY_SPEC, ANY_SPEC, VMEM_SPEC, VMEM_SPEC],
        out_specs=VMEM_SPEC,
        scratch_shapes=[
            pltpu.VMEM((TASKS, SHARD, HD), BF16),
            pltpu.VMEM((TASKS * GROUPS, 1, 128), F32),
            pltpu.VMEM((landed, HD), BF16),
            pltpu.VMEM((landed // 128, 1, 128), F32),
            pltpu.SemaphoreType.DMA((2,)),
            pltpu.SemaphoreType.DMA((hops,)),
            pltpu.SemaphoreType.DMA((hops,)),
            pltpu.SemaphoreType.DMA((hops,)),
            pltpu.SemaphoreType.DMA((hops,)),
        ],
        compiler_params=pltpu.CompilerParams(
            collective_id=1, has_side_effects=True, vmem_limit_bytes=48 * 2**20
        ),
        name="merge_parts",
    )(parts.reshape(TASKS, SHARD, HD), lams, own, own_lam)


def on_device(
    queries, prompt_keys, prompt_values, suffix_keys, suffix_values, new_keys, new_values,
    out_weight, span_perm, share_counts, sample_perm, decoded_lens,
):
    samples = sample_perm.shape[0]
    ids = jnp.arange(samples, dtype=jnp.int32)
    order = jnp.sum(jnp.where(sample_perm[None, :] == ids[:, None], ids[None, :], 0), axis=1)
    q = queries.reshape(SHARD, HD)
    q_all, own, own_lam = gather_queries(
        q, suffix_keys, suffix_values, new_keys, new_values, decoded_lens
    )
    parts, lams = attend_prompts(order, share_counts, span_perm, q_all, prompt_keys, prompt_values)
    attended = merge_parts(parts, lams, own, own_lam).astype(BF16).reshape(OWN * 3, 8 * HD)
    every_row = lax.all_gather(attended, "task", axis=0, tiled=True)
    return lax.psum_scatter(
        jnp.dot(every_row, out_weight, preferred_element_type=F32),
        "tp",
        scatter_dimension=0,
        tiled=True,
    )


def solution(mesh):
    return jax.shard_map(
        on_device,
        mesh=mesh,
        in_specs=(
            P("task", "tp"), P("task", "tp"), P("task", "tp"), P("task", "tp"), P("task", "tp"),
            P("task", "tp"), P("task", "tp"), P("tp", "task"), P("task"), P(), P(), P("task"),
        ),
        out_specs=P("tp", "task"),
        check_vma=False,
    )
```

time: 1960 us -> 305 us (0.16); the launches traced: 1930 us -> 300 us
  waiting for transfers between devices: 899 us -> 125 us
  other arithmetic: 536 us -> 1.86 us
  local copies, waits for them, and re-layouts: 341 us -> 7.98 us
  Pallas kernels: 0 us -> 146 us
  loops' own time: 84.6 us -> 0 us
  matrix products: 53.4 us -> 6.29 us
    scatter-add x50 -> x0, other arithmetic: 360 us -> none  [the longest x25 192 us: sum_block(): outputs = outputs.at[sample_ids].add(products, mode='drop')]
    unnamed x7 -> x2, waiting for transfers between devices: 271 us -> 0.03 us
    gather x77 -> x0, local copies, waits for them, and re-layouts: 240 us -> none  [the longest x50 172 us: block_scores(): picked = every_query[jnp.minimum(sample_ids, total_samples - 1)]]
    reduce_scatter x2 -> x1, waiting for transfers between devices: 271 us -> 33.7 us  [on_device(): lax.psum_scatter(jnp.dot(every_row, out_weight, preferred_element_type=F3...]
    pmax x1 -> x0, waiting for transfers between devices: 198 us -> none  [on_device(): maxima = lax.pmax(maxima, 'task')]
    another operation x27 -> x0, other arithmetic: 169 us -> none  [the longest x25 168 us: max_block(): return running.at[sample_ids].max(jnp.max(scores, axis=-1), mode='drop')]
    pallas_call x0 -> x3, Pallas kernels: none -> 146 us  [the longest x1 58.9 us: merge_parts(): pl.pallas_call(merge_kernel, out_shape=jax.ShapeDtypeStruct((SHARD, HD),...]
    another operation x34 -> x0, loops' own time: 84.6 us -> none  [the longest x1 42.8 us: on_device(): lax.fori_loop(0, slot_count, sum_slot, (zero_totals, zero_outputs))]
  transfers between devices with their start and end apart: 6 -> 2, of which waited for: 6 -> 2; matrix products, arithmetic and copies ran while one was open for 1% -> 0% of each run, Pallas kernels for 0% -> 0%
where the time goes in v1:
time: 305 us; the launch traced here: 300 us
  Pallas kernels  146 us (48%)
  waiting for transfers between devices  125 us (41%)
  between operations  13.4 us (4%)
  local copies, waits for them, and re-layouts  7.98 us (3%)
  matrix products  6.29 us (2%)
    all_gather x1, waiting for transfers between devices, on_device(): every_row = lax.all_gather(attended, 'task', axis=0, tiled=True)  91.2 us
    pallas_call x1, Pallas kernels, merge_parts(): pl.pallas_call(merge_kernel, out_shape=jax.ShapeDtypeStruct((SHARD, HD),...  58.9 us
    pallas_call x1, Pallas kernels, gather_queries(): pl.pallas_call(gather_kernel, out_shape=(jax.ShapeDtypeStruct((TASKS, SHA...  44.7 us
    pallas_call x1, Pallas kernels, attend_prompts(): pl.pallas_call(prompt_kernel, out_shape=(jax.ShapeDtypeStruct((rows, HD),...  42 us
    reduce_scatter x1, waiting for transfers between devices, on_device(): lax.psum_scatter(jnp.dot(every_row, out_weight, preferred_element_type=F3...  33.7 us
    dot_general x1, matrix products, on_device(): jnp.dot(every_row, out_weight, preferred_element_type=F32)  6.29 us
    unnamed x14, local copies, waits for them, and re-layouts  6.2 us
  transfers between devices with their start and end apart: 2, of which 2 were waited for; matrix products, arithmetic and copies ran while one was open for 0% of the time, Pallas kernels for 0%

profile of v1, /device:TPU:49, one launch (start us, length us, event | category | flops | bytes accessed | tf_op | source)
XLA Modules:
  0.0 300.0 jit_solution(12036035912154128671)
XLA Ops:
  6.5 0.0 copy-start
  6.5 0.0 all-gather.2.cloned.1.call-start
  6.5 1.8 select_reduce_fusion.order_ref
  8.4 1.0 reshape.13.q_ref
  9.4 0.0 copy-start.1
  9.4 1.6 copy-done.1
  11.0 0.0 copy-start.2
  11.0 1.6 copy-done.2
  12.6 0.0 copy-start.4
  12.6 0.7 copy-done.4
  13.3 0.7 copy-done.5
  14.1 0.7 copy-done.6
  14.7 44.7 %gather_queries.1 = (bf16[32,768,128]{2,1,0:T(8,128)(2,1)}, f32[768,128]{1,0:T(8,128)S(1)}, f32[6,1,128]{2,1,0:T(1,128)S(1)}) custom-call(bf16[768,128]{1,0:T(8,128)(2,1)S(1)} %reshape.13.q_ref, bf16[8192,128]{1,0:T(8,128)(2,1)S(1)} %copy-done.1, bf16[8192,128]{1,0:T(8,128)(2,1)S(1)} %copy-done.2, bf16[96,128]{1,0:T(8,128)(2,1)S(1)} %copy-done.4, ...), custom_call_target="tpu_custom_call" | custom-call | tf_op jit(solution)/shard_map/gather_queries/pallas_call | solution.py:195
  59.4 42.0 %attend_prompts.1 = (bf16[24576,128]{1,0:T(8,128)(2,1)}, f32[192,1,128]{2,1,0:T(1,128)}) custom-call(s32[1024]{0:T(1024)} %select_reduce_fusion.order_ref, s32[16]{0:T(128)} %counts_ref.1, s32[16]{0:T(128)} %span_ref.1, bf16[24576,128]{1,0:T(8,128)(2,1)} %bitcast.4, bf16[4096,128]{1,0:T(8,128)(2,1)} %k_ref.1, bf16[4096,128]{1,0:T(8,128)(2,1)} %v_ref.1), custom_call_target="tpu_custom_call" | custom-call | tf_op jit(solution)/shard_map/attend_prompts/pallas_call | solution.py:314
  101.4 0.9 copy-done.3
  102.3 58.9 %merge_parts.1 = f32[768,128]{1,0:T(8,128)S(1)} custom-call(bf16[32,768,128]{2,1,0:T(8,128)(2,1)} %bitcast.5, f32[192,1,128]{2,1,0:T(1,128)S(1)} %copy-done.3, f32[768,128]{1,0:T(8,128)S(1)} %get-tuple-element.13.own_ref, f32[6,1,128]{2,1,0:T(1,128)S(1)} %get-tuple-element.14.own_lam_ref), custom_call_target="tpu_custom_call" | custom-call | tf_op jit(solution)/shard_map/merge_parts/pallas_call | solution.py:424
  161.2 0.8 reshape.16
  161.9 0.0 all-gather.2.cloned.1.call-update
  162.0 0.0 reduce-scatter.2.cloned.1.call-start
  162.0 91.2 %all-gather.2.cloned.1.call-done = bf16[3072,1024]{1,0:T(8,128)(2,1)} async-done(((bf16[96,1024]{1,0:T(8,128)(2,1)}), bf16[3072,1024]{1,0:T(8,128)(2,1)}) %all-gather.2.cloned.1.call-update) | async-done | bytes 6291472 | tf_op jit(solution)/shard_map/all_gather | solution.py:460
  253.2 0.0 copy-done
  253.2 6.3 %fusion = f32[3072,256]{1,0:T(8,128)} fusion(bf16[3072,1024]{1,0:T(8,128)(2,1)} %all-gather.2.cloned.1.call-done, bf16[1024,256]{1,0:T(8,128)(2,1)S(1)} %copy-done), kind=kOutput, calls=%fused_computation.2 | convolution fusion | flops 1610612736 | bytes 9961472 | tf_op jit(solution)/shard_map/dot_general | solution.py:462
  259.5 0.0 reduce-scatter.2.cloned.1.call-update
  259.5 33.7 %reduce-scatter.2.cloned.1.call-done = f32[384,256]{1,0:T(8,128)} async-done(((f32[3072,256]{1,0:T(8,128)}), f32[384,256]{1,0:T(8,128)}) %reduce-scatter.2.cloned.1.call-update) | async-done | bytes 393232 | tf_op jit(solution)/shard_map/reduce_scatter | solution.py:461
  (4 shorter events, 0.0 us)
Async XLA Ops:
  6.5 246.7 %copy-start = (bf16[1024,256]{1,0:T(8,128)(2,1)S(1)}, bf16[1024,256]{1,0:T(8,128)(2,1)}, u32[]{:S(2)}) copy-start(bf16[1024,256]{1,0:T(8,128)(2,1)} %param.19) | copy-start | bytes 1572868
  6.5 246.7 %all-gather.2.cloned.1.call-start = ((), (), s32[]{:S(2)}) async-start(), calls=%async_computation.1 | async-start | bytes 6488064 | tf_op jit(solution)/shard_map/all_gather | solution.py:460
  9.4 1.6 copy-start.1
  11.0 1.6 copy-start.2
  12.6 0.7 copy-start.4
  13.3 0.7 copy-start.5
  14.1 0.7 copy-start.6
  101.4 0.9 copy-start.3
  162.0 131.2 %reduce-scatter.2.cloned.1.call-start = ((), (), s32[]{:S(2)}) async-start(), calls=%async_computation.2 | async-start | bytes 3538944 | tf_op jit(solution)/shard_map/reduce_scatter | solution.py:461
Sparse Core Ops, SparseCore 0:
  162.1 91.0 all-gather.1
  259.6 33.4 reduce-scatter.1

commit v2 on v1

--- a/solution.py
+++ b/solution.py
@@ -98,13 +98,15 @@
     return lax.rem(z + 2 * NZ, NZ) * NX + lax.rem(x + 2 * NX, NX)
 
 
-def greet_neighbours(z, x):
+def greet(devices):
     barrier = pltpu.get_barrier_semaphore()
-    for dz, dx in ((1, 0), (-1, 0), (0, 1), (0, -1)):
-        pl.semaphore_signal(
-            barrier, inc=1, device_id={"task": task_at(z + dz, x + dx)}, device_id_type=MESH_ID
-        )
-    pl.semaphore_wait(barrier, 4)
+    for device in devices:
+        pl.semaphore_signal(barrier, inc=1, device_id=device, device_id_type=MESH_ID)
+    pl.semaphore_wait(barrier, len(devices))
+
+
+def plane_neighbours(z, x):
+    return [{"task": task_at(z + dz, x + dx)} for dz, dx in ((1, 0), (-1, 0), (0, 1), (0, -1))]
 
 
 def suffix_pair(pair, q_ref, sk_ref, sv_ref, nk_ref, nv_ref, lens_ref, o_ref, lam_ref):
@@ -146,7 +148,7 @@
     wide_ref, own_sem, send_sems, recv_sems,
 ):
     z, x = place()
-    greet_neighbours(z, x)
+    greet(plane_neighbours(z, x))
     own = pltpu.make_async_copy(q_ref, all_ref.at[task_at(z, x)], own_sem)
     own.start()
 
@@ -334,15 +336,21 @@
 
 
 def merge_kernel(
-    part_in, lam_in, own_ref, own_lam_ref, out_ref,
-    part_ref, lam_ref, land_ref, lland_ref, in_sem, send_sems, recv_sems, lsend_sems, lrecv_sems,
+    part_in, lam_in, own_ref, own_lam_ref, w_ref, out_ref,
+    part_ref, lam_ref, land_ref, lland_ref, mix_ref, a_ref, p_ref, c_ref, y_ref, yland_ref, r_ref,
+    in_sem, send_sems, recv_sems, lsend_sems, lrecv_sems,
+    a_sems, c_sems, y_sems, x_sems,
 ):
     z, x = place()
+    tp = lax.axis_index("tp")
+    y, core = tp // 2, lax.rem(tp, 2)
+    partner = {"tp": 2 * y + 1 - core}
+    up, down = ({"tp": 2 * lax.rem(y + d, 4) + core} for d in (1, 3))
     load = pltpu.make_async_copy(part_in, part_ref, in_sem.at[0])
     lload = pltpu.make_async_copy(lam_in, lam_ref, in_sem.at[1])
     load.start()
     lload.start()
-    greet_neighbours(z, x)
+    greet(plane_neighbours(z, x) + [{"task": task_at(z, x + 2)}, partner, up, down])
     load.wait()
     lload.wait()
     offsets, at = {}, 0
@@ -402,7 +410,7 @@
                 weight = jnp.transpose(jnp.broadcast_to(share / total, (128, 128)))
                 mixed = mixed + weight * (part - parts[0])
             if last:
-                out_ref[pl.ds(128 * g, 128), :] = mixed
+                mix_ref[pl.ds(128 * g, 128), :] = mixed
             else:
                 lam_ref[origin * GROUPS + g] = top + jnp.log(total)
                 part_ref[origin, pl.ds(128 * g, 128), :] = mixed.astype(BF16)
@@ -417,31 +425,170 @@
         for copy in copies(hop):
             copy.wait_send()
 
-
-def merge_parts(parts, lams, own, own_lam):
+    def remote(src, dst, sems, index, device):
+        return pltpu.make_async_remote_copy(
+            src_ref=src, dst_ref=dst, send_sem=sems.at[0, index], recv_sem=sems.at[1, index],
+            device_id=device, device_id_type=MESH_ID,
+        )
+
+    for g in range(8):
+        a_ref[pl.ds(0, 96), pl.ds(128 * g, 128)] = mix_ref[
+            pl.ds(g, 96, stride=8), :
+        ].astype(BF16)
+    slot_of = {0: 0, 1: 1, -1: 2, 2: 3, -2: 4, 3: 5, -3: 6, 4: 7, -4: 7}
+
+    def row_copy(way, step, half):
+        src = pl.ds(96 * slot_of[way * (step - 1)] + 48 * half, 48)
+        dst = pl.ds(96 * slot_of[way * step] + 48 * half, 48)
+        index = (step - 1) * 4 + (0 if way == 1 else 2) + half
+        return remote(
+            a_ref.at[src], a_ref.at[dst], a_sems, index, {"task": task_at(z + way, x)}
+        )
+
+    hops = [
+        (way, step, half)
+        for step in range(1, 5)
+        for half in (0, 1)
+        for way in (1, -1)
+        if step < 4 or half == (0 if way == 1 else 1)
+    ]
+
+    def block_of(offset):
+        return lax.rem(z - offset + NZ, NZ)
+
+    def hand_over(offset):
+        block = block_of(offset)
+        return lax.rem(block, 2) != core, remote(
+            p_ref.at[block], c_ref.at[slot_of[offset]], c_sems, slot_of[offset], partner
+        )
+
+    def project(offsets):
+        first = slot_of[offsets[0]]
+        rows = a_ref[pl.ds(96 * first, 96 * len(offsets)), :]
+        for q in range(NX):
+            product = jnp.dot(rows, w_ref[q], preferred_element_type=F32)
+            for i, offset in enumerate(offsets):
+                p_ref[block_of(offset), :, pl.ds(256 * q, 256)] = product[96 * i : 96 * i + 96]
+        for offset in offsets:
+            away, copy = hand_over(offset)
+
+            @pl.when(away)
+            def _():
+                copy.start()
+
+    def take_over(offsets):
+        for offset in offsets:
+            away, copy = hand_over(offset)
+
+            @pl.when(jnp.logical_not(away))
+            def _():
+                copy.wait_recv()
+                block = block_of(offset)
+                p_ref[block] = p_ref[block] + c_ref[slot_of[offset]]
+
+    for hop in hops:
+        if hop[1] == 1:
+            row_copy(*hop).start()
+    turns = [[0], [1, -1], [2, -2], [3, -3], [4]]
+    for step, offsets in enumerate(turns):
+        for hop in hops:
+            if hop[1] == step:
+                row_copy(*hop).wait_recv()
+                onward = (hop[0], step + 1, hop[2])
+                if onward in hops:
+                    row_copy(*onward).start()
+        project(offsets)
+        if step:
+            take_over(turns[step - 1])
+    take_over(turns[-1])
+
+    def tp_block(d):
+        return 2 * lax.rem(y + d, 4) + core
+
+    top, low = pl.ds(0, 48), pl.ds(48, 48)
+    far, plus, minus = tp_block(2), tp_block(1), tp_block(3)
+    y_ref[0] = p_ref[far].astype(BF16)
+    y_ref[1, low] = p_ref[plus, pl.ds(48, 48), :].astype(BF16)
+    y_ref[2, top] = p_ref[minus, pl.ds(0, 48), :].astype(BF16)
+    relay_up = remote(y_ref.at[0, top], yland_ref.at[0, top], y_sems, 0, up)
+    relay_down = remote(y_ref.at[0, low], yland_ref.at[0, low], y_sems, 1, down)
+    early_up = remote(y_ref.at[1, low], yland_ref.at[1, low], y_sems, 2, up)
+    early_down = remote(y_ref.at[2, top], yland_ref.at[2, top], y_sems, 3, down)
+    late_up = remote(y_ref.at[1, top], yland_ref.at[1, top], y_sems, 4, up)
+    late_down = remote(y_ref.at[2, low], yland_ref.at[2, low], y_sems, 5, down)
+    for copy in (relay_up, relay_down, early_up, early_down):
+        copy.start()
+    relay_up.wait_recv()
+    y_ref[1, top] = (p_ref[plus, pl.ds(0, 48), :] + yland_ref[0, top].astype(F32)).astype(BF16)
+    late_up.start()
+    relay_down.wait_recv()
+    y_ref[2, low] = (p_ref[minus, pl.ds(48, 48), :] + yland_ref[0, low].astype(F32)).astype(BF16)
+    late_down.start()
+    for copy in (early_up, early_down, late_up, late_down):
+        copy.wait_recv()
+    mine = p_ref[tp_block(0)] + yland_ref[1].astype(F32) + yland_ref[2].astype(F32)
+    for q in range(NX):
+        r_ref[q] = mine[:, 256 * q : 256 * q + 256]
+
+    shares = []
+    for d in (1, 2, 3):
+        peer = lax.rem(x + d, NX)
+        share = remote(
+            r_ref.at[peer], out_ref.at[x], x_sems, d - 1, {"task": task_at(z, peer)}
+        )
+        share.start()
+        shares.append(share)
+    out_ref[x] = r_ref[x]
+    for share in shares:
+        share.wait_recv()
+    for share in shares + [relay_up, relay_down, early_up, early_down, late_up, late_down]:
+        share.wait_send()
+    for hop in hops:
+        row_copy(*hop).wait_send()
+    for offset in slot_of:
+        if offset > -4:
+            away, copy = hand_over(offset)
+
+            @pl.when(away)
+            def _():
+                copy.wait_send()
+
+
+def merge_parts(parts, lams, own, own_lam, weights):
     hops = len(TREE)
     landed = sum(hop.high - hop.low for hop in TREE)
     return pl.pallas_call(
         merge_kernel,
-        out_shape=jax.ShapeDtypeStruct((SHARD, HD), F32),
-        in_specs=[ANY_SPEC, ANY_SPEC, VMEM_SPEC, VMEM_SPEC],
+        out_shape=jax.ShapeDtypeStruct((NX, 96, 256), F32),
+        in_specs=[ANY_SPEC, ANY_SPEC, VMEM_SPEC, VMEM_SPEC, VMEM_SPEC],
         out_specs=VMEM_SPEC,
         scratch_shapes=[
             pltpu.VMEM((TASKS, SHARD, HD), BF16),
             pltpu.VMEM((TASKS * GROUPS, 1, 128), F32),
             pltpu.VMEM((landed, HD), BF16),
             pltpu.VMEM((landed // 128, 1, 128), F32),
+            pltpu.VMEM((SHARD, HD), F32),
+            pltpu.VMEM((8 * 96, 1024), BF16),
+            pltpu.VMEM((8, 96, 1024), F32),
+            pltpu.VMEM((8, 96, 1024), F32),
+            pltpu.VMEM((3, 96, 1024), BF16),
+            pltpu.VMEM((3, 96, 1024), BF16),
+            pltpu.VMEM((NX, 96, 256), F32),
             pltpu.SemaphoreType.DMA((2,)),
             pltpu.SemaphoreType.DMA((hops,)),
             pltpu.SemaphoreType.DMA((hops,)),
             pltpu.SemaphoreType.DMA((hops,)),
             pltpu.SemaphoreType.DMA((hops,)),
+            pltpu.SemaphoreType.DMA((2, 16)),
+            pltpu.SemaphoreType.DMA((2, 8)),
+            pltpu.SemaphoreType.DMA((2, 6)),
+            pltpu.SemaphoreType.DMA((2, 3)),
         ],
         compiler_params=pltpu.CompilerParams(
-            collective_id=1, has_side_effects=True, vmem_limit_bytes=48 * 2**20
+            collective_id=1, has_side_effects=True, vmem_limit_bytes=56 * 2**20
         ),
         name="merge_parts",
-    )(parts.reshape(TASKS, SHARD, HD), lams, own, own_lam)
+    )(parts.reshape(TASKS, SHARD, HD), lams, own, own_lam, weights)
 
 
 def on_device(
@@ -455,15 +602,11 @@
     q_all, own, own_lam = gather_queries(
         q, suffix_keys, suffix_values, new_keys, new_values, decoded_lens
     )
+    weight, q_all = lax.optimization_barrier((out_weight, q_all))
+    rings = [[NX * z + x for x in range(NX)] for z in range(NZ)]
+    weights = lax.all_gather(weight, "task", axis_index_groups=rings)
     parts, lams = attend_prompts(order, share_counts, span_perm, q_all, prompt_keys, prompt_values)
-    attended = merge_parts(parts, lams, own, own_lam).astype(BF16).reshape(OWN * 3, 8 * HD)
-    every_row = lax.all_gather(attended, "task", axis=0, tiled=True)
-    return lax.psum_scatter(
-        jnp.dot(every_row, out_weight, preferred_element_type=F32),
-        "tp",
-        scatter_dimension=0,
-        tiled=True,
-    )
+    return merge_parts(parts, lams, own, own_lam, weights).reshape(NX * 96, 256)
 
 
 def solution(mesh):

time: 305 us -> 220 us (0.72)
  waiting for transfers between devices: 125 us -> 0.02 us
  Pallas kernels: 146 us -> 194 us
  matrix products: 6.29 us -> 0 us
    all_gather x1, waiting for transfers between devices: 91.2 us -> 0.01 us  [on_device(): weights = lax.all_gather(weight, 'task', axis_index_groups=rings)]
    pallas_call x1, Pallas kernels: 58.9 us -> 97.7 us  [merge_parts(): pl.pallas_call(merge_kernel, out_shape=jax.ShapeDtypeStruct((NX, 96, 256)...]
    reduce_scatter x1 -> x0, waiting for transfers between devices: 33.7 us -> none  [on_device(): lax.psum_scatter(jnp.dot(every_row, out_weight, preferred_element_type=F3...]
    pallas_call x1, Pallas kernels: 42 us -> 51.7 us  [attend_prompts(): pl.pallas_call(prompt_kernel, out_shape=(jax.ShapeDtypeStruct((rows, HD),...]
    dot_general x1 -> x0, matrix products: 6.29 us -> none  [on_device(): jnp.dot(every_row, out_weight, preferred_element_type=F32)]
    unnamed x14 -> x17, local copies, waits for them, and re-layouts: 6.2 us -> 8.41 us
  transfers between devices with their start and end apart: 2 -> 1, of which waited for: 2 -> 0; matrix products, arithmetic and copies ran while one was open for 0% -> 1% of each run, Pallas kernels for 0% -> 24%
where the time goes in v2:
time: 220 us; the launch traced here: 218 us
  Pallas kernels  194 us (88%)
  between operations  13.4 us (6%)
  local copies, waits for them, and re-layouts  9.43 us (4%)
    pallas_call x1, Pallas kernels, merge_parts(): pl.pallas_call(merge_kernel, out_shape=jax.ShapeDtypeStruct((NX, 96, 256)...  97.7 us
    pallas_call x1, Pallas kernels, attend_prompts(): pl.pallas_call(prompt_kernel, out_shape=(jax.ShapeDtypeStruct((rows, HD),...  51.7 us
    pallas_call x1, Pallas kernels, gather_queries(): pl.pallas_call(gather_kernel, out_shape=(jax.ShapeDtypeStruct((TASKS, SHA...  44.7 us
    unnamed x17, local copies, waits for them, and re-layouts  8.41 us
  transfers between devices with their start and end apart: 1, of which 0 were waited for; matrix products, arithmetic and copies ran while one was open for 1% of the time, Pallas kernels for 24%

profile of v2, /device:TPU:49, one launch (start us, length us, event | category | flops | bytes accessed | tf_op | source)
XLA Modules:
  0.0 218.0 jit_solution(2610617849600574416)
XLA Ops:
  6.5 0.0 copy-start.7
  6.5 0.0 all-gather.3.cloned.1.call-start
  6.5 1.0 reshape.13.q_ref
  7.6 0.0 copy-start
  7.6 1.6 copy-done
  9.2 0.0 copy-start.1
  9.2 1.6 copy-done.1
  10.8 0.0 copy-start.3
  10.8 0.7 copy-done.3
  11.5 0.0 copy-start.4
  11.5 0.7 copy-done.4
  12.2 0.0 copy-start.6
  12.2 0.7 copy-done.6
  12.9 44.7 %gather_queries.1 = (bf16[32,768,128]{2,1,0:T(8,128)(2,1)}, f32[768,128]{1,0:T(8,128)S(1)}, f32[6,1,128]{2,1,0:T(1,128)S(1)}) custom-call(bf16[768,128]{1,0:T(8,128)(2,1)S(1)} %reshape.13.q_ref, bf16[8192,128]{1,0:T(8,128)(2,1)S(1)} %copy-done, bf16[8192,128]{1,0:T(8,128)(2,1)S(1)} %copy-done.1, bf16[96,128]{1,0:T(8,128)(2,1)S(1)} %copy-done.3, ...), custom_call_target="tpu_custom_call" | custom-call | tf_op jit(solution)/shard_map/gather_queries/pallas_call | solution.py:197
  57.6 0.0 copy-start.2
  57.6 0.7 copy-done.2
  58.3 0.0 copy-start.5
  58.3 0.6 copy-done.5
  58.9 0.0 all-gather.3.cloned.1.call-update
  58.9 0.0 copy-done.7
  58.9 1.1 select_reduce_fusion.order_ref
  60.0 51.7 %attend_prompts.1 = (bf16[24576,128]{1,0:T(8,128)(2,1)}, f32[192,1,128]{2,1,0:T(1,128)}) custom-call(s32[1024]{0:T(1024)} %select_reduce_fusion.order_ref, s32[16]{0:T(128)} %counts_ref.1, s32[16]{0:T(128)} %span_ref.1, bf16[24576,128]{1,0:T(8,128)(2,1)} %bitcast.4, bf16[4096,128]{1,0:T(8,128)(2,1)} %k_ref.1, bf16[4096,128]{1,0:T(8,128)(2,1)} %v_ref.1), custom_call_target="tpu_custom_call" | custom-call | tf_op jit(solution)/shard_map/attend_prompts/pallas_call | solution.py:316
  111.7 97.7 %merge_parts.1 = f32[4,96,256]{2,1,0:T(8,128)} custom-call(bf16[32,768,128]{2,1,0:T(8,128)(2,1)} %bitcast.5, f32[192,1,128]{2,1,0:T(1,128)} %get-tuple-element.15.lam_in, f32[768,128]{1,0:T(8,128)} %copy-done.2, f32[6,1,128]{2,1,0:T(1,128)} %copy-done.5, bf16[4,1024,256]{2,1,0:T(8,128)(2,1)} %bitcast.6), custom_call_target="tpu_custom_call" | custom-call | tf_op jit(solution)/shard_map/merge_parts/pallas_call | solution.py:560
  209.4 1.8 copy.14
  (1 shorter events, 0.0 us)
Async XLA Ops:
  6.5 52.4 %copy-start.7 = (s32[1024]{0:T(1024)S(1)}, s32[1024]{0:T(1024)}, u32[]{:S(2)}) copy-start(s32[1024]{0:T(1024)} %param.22) | copy-start | bytes 12292
  6.5 105.2 %all-gather.3.cloned.1.call-start = ((), (), s32[]{:S(2)}) async-start(), calls=%async_computation | async-start | bytes 2621440 | tf_op jit(solution)/shard_map/all_gather | solution.py:607
  7.6 1.6 copy-start
  9.2 1.6 copy-start.1
  10.8 0.7 copy-start.3
  11.5 0.7 copy-start.4
  12.2 0.7 copy-start.6
  57.6 0.7 copy-start.2
  58.3 0.6 copy-start.5
Sparse Core Ops, SparseCore 0:
  59.0 36.8 all-gather.2

commit v3 on v2

--- a/solution.py
+++ b/solution.py
@@ -19,7 +19,7 @@
 TASKS = NZ * NX
 SHARD = 768
 OWN = 32
-CHUNK = 16
+CHUNK = 160
 ROWS = CHUNK * 24
 SLOTS = 16
 GROUPS = SHARD // 128
@@ -29,7 +29,6 @@
 BF16 = jnp.bfloat16
 LOG2E = math.log2(math.e)
 SCALE = 1.0 / math.sqrt(HD)
-XROWS = 256
 
 
 class Hop:
@@ -39,7 +38,7 @@
         self.kids = []
 
 
-def gather_tree():
+def gather_tree(split):
     hops = []
 
     def add(axis, way, dz, dx, rows, deps):
@@ -62,7 +61,7 @@
             held.setdefault(far, []).append(add(axis, way, place[0], place[1], half, deps))
         return held
 
-    rows_x, rows_z = (0, XROWS), (XROWS, SHARD)
+    rows_x, rows_z = (0, split), (split, SHARD)
     for dx, base in ring("x", NX, rows_x, [], 0, 0).items():
         ring("z", NZ, rows_x, base, 0, dx)
     for dz, base in ring("z", NZ, rows_z, [], 0, 0).items():
@@ -86,7 +85,8 @@
     return sorted(hops, key=lambda hop: arrival[hop.index])
 
 
-TREE = gather_tree()
+TREE = gather_tree(320)
+BACK = gather_tree(256)
 
 
 def place():
@@ -145,11 +145,20 @@
 
 def gather_kernel(
     q_ref, sk_ref, sv_ref, nk_ref, nv_ref, lens_ref, all_ref, o_ref, lam_ref,
-    wide_ref, own_sem, send_sems, recv_sems,
+    wide_ref, skv_ref, own_sem, send_sems, recv_sems,
 ):
     z, x = place()
+    loads = []
+    for quarter in range(4):
+        rows = pl.ds(quarter * 2048, 2048)
+        for i, ref in enumerate((sk_ref, sv_ref)):
+            load = pltpu.make_async_copy(
+                ref.at[rows], skv_ref.at[i, rows], own_sem.at[2 * quarter + i]
+            )
+            load.start()
+            loads.append(load)
     greet(plane_neighbours(z, x))
-    own = pltpu.make_async_copy(q_ref, all_ref.at[task_at(z, x)], own_sem)
+    own = pltpu.make_async_copy(q_ref, all_ref.at[task_at(z, x)], own_sem.at[8])
     own.start()
 
     def copy(hop):
@@ -173,7 +182,10 @@
     pair = 0
     for count, hop in enumerate(TREE):
         if count % 4 == 0 and pair < OWN // 2:
-            suffix_pair(pair, q_ref, sk_ref, sv_ref, nk_ref, nv_ref, lens_ref, o_ref, wide_ref)
+            if pair % 4 == 0:
+                loads[pair // 2].wait()
+                loads[pair // 2 + 1].wait()
+            suffix_pair(pair, q_ref, skv_ref.at[0], skv_ref.at[1], nk_ref, nv_ref, lens_ref, o_ref, wide_ref)
             pair += 1
         copy(hop).wait_recv()
         done.add(hop.index)
@@ -190,6 +202,7 @@
 VMEM_SPEC = pl.BlockSpec(memory_space=pltpu.VMEM)
 SMEM_SPEC = pl.BlockSpec(memory_space=pltpu.SMEM)
 ANY_SPEC = pl.BlockSpec(memory_space=pl.ANY)
+HBM_SPEC = pl.BlockSpec(memory_space=pltpu.HBM)
 
 
 def gather_queries(q, suffix_keys, suffix_values, new_keys, new_values, lens):
@@ -201,16 +214,17 @@
             jax.ShapeDtypeStruct((SHARD, HD), F32),
             jax.ShapeDtypeStruct((GROUPS, 1, 128), F32),
         ),
-        in_specs=[VMEM_SPEC] * 5 + [SMEM_SPEC],
+        in_specs=[VMEM_SPEC, HBM_SPEC, HBM_SPEC, VMEM_SPEC, VMEM_SPEC, SMEM_SPEC],
         out_specs=(ANY_SPEC, VMEM_SPEC, VMEM_SPEC),
         scratch_shapes=[
             pltpu.VMEM((SHARD, 128), F32),
-            pltpu.SemaphoreType.DMA,
+            pltpu.VMEM((2, OWN * SUF, HD), BF16),
+            pltpu.SemaphoreType.DMA((9,)),
             pltpu.SemaphoreType.DMA((hops,)),
             pltpu.SemaphoreType.DMA((hops,)),
         ],
         compiler_params=pltpu.CompilerParams(
-            collective_id=0, has_side_effects=True, vmem_limit_bytes=48 * 2**20
+            collective_id=0, has_side_effects=True, vmem_limit_bytes=62 * 2**20
         ),
         name="gather_queries",
     )(q, suffix_keys, suffix_values, new_keys, new_values, lens)
@@ -218,7 +232,7 @@
 
 def prompt_kernel(
     order_ref, counts_ref, span_ref, q_ref, k_ref, v_ref, out_ref, lam_ref,
-    o_ref, wide_ref, qs_ref, acc_ref, top_ref, blocks_ref, have_ref,
+    o_ref, wide_ref, qs_ref, acc_ref, top_ref, stage_ref, blocks_ref, have_ref, out_sems,
 ):
     for p in range(16):
         have_ref[p] = 0
@@ -239,48 +253,87 @@
 
         lax.fori_loop(0, count, one, 0)
 
+    def chunk(p, base, end, size):
+        have = have_ref[p]
+        rows = pl.ds(0, 24 * size)
+        samples = [order_ref[jnp.minimum(base + i, end - 1)] for i in range(size)]
+        for i, s in enumerate(samples):
+            at = pl.multiple_of((s >> 1) * 48, 16)
+            both = q_ref[pl.ds(at, 48), :].astype(F32)
+            qs_ref[pl.ds(24 * i, 24), :] = jnp.where((s & 1) == 1, both[24:48], both[0:24])
+
+        def scores(b):
+            at = pl.multiple_of(blocks_ref[p * SLOTS + b] * SPAN, SPAN)
+            keys = k_ref[pl.ds(at, SPAN), :]
+            values = jnp.concatenate([v_ref[pl.ds(at, SPAN), :], ones], axis=1)
+            q = qs_ref[rows, :].astype(BF16)
+            return values, lax.dot_general(q, keys, nt, preferred_element_type=F32)
+
+        def weigh(s, top):
+            return jnp.exp2((s - top) * (SCALE * LOG2E)).astype(BF16)
+
+        values, s = scores(0)
+        top = jnp.max(s, axis=-1, keepdims=True)
+        acc_ref[rows, :] = jnp.dot(weigh(s, top), values, preferred_element_type=F32)
+        top_ref[rows, :] = jnp.broadcast_to(top, (24 * size, 128))
+
+        def block(b, inner):
+            values, s = scores(b)
+            old = top_ref[rows, :]
+            top = jnp.maximum(old, jnp.max(s, axis=-1, keepdims=True))
+            w = weigh(s, jnp.concatenate([top, top], axis=1))
+            decay = jnp.exp2((old - top) * (SCALE * LOG2E))
+            acc_ref[rows, :] = acc_ref[rows, :] * jnp.concatenate(
+                [decay, decay], axis=1
+            ) + jnp.dot(w, values, preferred_element_type=F32)
+            top_ref[rows, :] = top
+            return inner
+
+        lax.fori_loop(1, have, block, 0)
+        for i, s in enumerate(samples):
+            here = pl.ds(24 * i, 24)
+            total = acc_ref[here, pl.ds(128, 128)]
+            at = pl.multiple_of(s * 24, 8)
+            o_ref[pl.ds(at, 24), :] = acc_ref[here, pl.ds(0, 128)] / total
+            wide_ref[pl.ds(at, 24), :] = top_ref[here, :] * SCALE + jnp.log(total)
+
     def attend(p, first, count):
-        have = have_ref[p]
-
-        def chunk(c, carry):
-            base = first + c * CHUNK
-            samples = [order_ref[jnp.minimum(base + i, first + count - 1)] for i in range(CHUNK)]
-            for i, s in enumerate(samples):
-                at = pl.multiple_of((s >> 1) * 48, 16)
-                both = q_ref[pl.ds(at, 48), :].astype(F32)
-                qs_ref[pl.ds(24 * i, 24), :] = jnp.where((s & 1) == 1, both[24:48], both[0:24])
-            top_ref[...] = jnp.full((ROWS, 128), LOWEST, F32)
-            acc_ref[...] = jnp.zeros((ROWS, 256), F32)
-
-            def block(b, inner):
-                slot = blocks_ref[p * SLOTS + b]
-                at = pl.multiple_of(slot * SPAN, SPAN)
-                keys = k_ref[pl.ds(at, SPAN), :]
-                values = jnp.concatenate([v_ref[pl.ds(at, SPAN), :], ones], axis=1)
-                for part in range(3):
-                    rows = pl.ds(128 * part, 128)
-                    q = qs_ref[rows, :].astype(BF16)
-                    s = lax.dot_general(q, keys, nt, preferred_element_type=F32) * (SCALE * LOG2E)
-                    old = top_ref[rows, :]
-                    new = jnp.maximum(old, jnp.max(s, axis=-1, keepdims=True))
-                    w = jnp.exp2(s - jnp.concatenate([new, new], axis=1)).astype(BF16)
-                    decay = jnp.exp2(old - new)
-                    acc_ref[rows, :] = acc_ref[rows, :] * jnp.concatenate(
-                        [decay, decay], axis=1
-                    ) + jnp.dot(w, values, preferred_element_type=F32)
-                    top_ref[rows, :] = new
-                return inner
-
-            lax.fori_loop(0, have, block, 0)
-            for i, s in enumerate(samples):
-                rows = pl.ds(24 * i, 24)
-                total = acc_ref[rows, pl.ds(128, 128)]
-                at = pl.multiple_of(s * 24, 8)
-                o_ref[pl.ds(at, 24), :] = acc_ref[rows, pl.ds(0, 128)] / total
-                wide_ref[pl.ds(at, 24), :] = top_ref[rows, :] * (1.0 / LOG2E) + jnp.log(total)
+        full = count // CHUNK
+
+        def whole(c, carry):
+            chunk(p, first + c * CHUNK, first + count, CHUNK)
             return carry
 
-        lax.fori_loop(0, (count + CHUNK - 1) // CHUNK, chunk, 0)
+        lax.fori_loop(0, full, whole, 0)
+        rest = count - full * CHUNK
+
+        @pl.when((rest > 128) & (rest <= 160))
+        def _():
+            chunk(p, first + full * CHUNK, first + count, 160)
+
+        @pl.when((rest > 96) & (rest <= 128))
+        def _():
+            chunk(p, first + full * CHUNK, first + count, 128)
+
+        @pl.when((rest > 64) & (rest <= 96))
+        def _():
+            chunk(p, first + full * CHUNK, first + count, 96)
+
+        @pl.when((rest > 48) & (rest <= 64))
+        def _():
+            chunk(p, first + full * CHUNK, first + count, 64)
+
+        @pl.when((rest > 32) & (rest <= 48))
+        def _():
+            chunk(p, first + full * CHUNK, first + count, 48)
+
+        @pl.when((rest > 16) & (rest <= 32))
+        def _():
+            chunk(p, first + full * CHUNK, first + count, 32)
+
+        @pl.when((rest > 0) & (rest <= 16))
+        def _():
+            chunk(p, first + full * CHUNK, first + count, 16)
 
     def prompt(p, first):
         count = counts_ref[p]
@@ -297,18 +350,32 @@
 
     lax.fori_loop(0, 16, prompt, 0)
 
+    lane = lax.broadcasted_iota(jnp.int32, (8, 128), 1)
+    corner = (lane & 7) == lax.broadcasted_iota(jnp.int32, (8, 128), 0)
+
+    def put(plane):
+        tasks = pl.ds(plane * NX, NX)
+        return pltpu.make_async_copy(stage_ref.at[tasks], out_ref.at[tasks], out_sems.at[plane])
+
     def finish(t, carry):
         at = pl.multiple_of(t * SHARD, SHARD)
-        out_ref[pl.ds(at, SHARD), :] = o_ref[pl.ds(at, SHARD), :].astype(BF16)
-        eye = lax.broadcasted_iota(jnp.int32, (128, 128), 0) == lax.broadcasted_iota(
-            jnp.int32, (128, 128), 1
-        )
+        stage_ref[t] = o_ref[pl.ds(at, SHARD), :].astype(BF16)
+
+        @pl.when((t & 3) == 3)
+        def _():
+            put(t >> 2).start()
+
         for g in range(GROUPS):
             tile = wide_ref[pl.ds(pl.multiple_of(at + 128 * g, 128), 128), :]
-            lam_ref[t * GROUPS + g] = jnp.sum(jnp.where(eye, tile, 0.0), axis=0, keepdims=True)
+            row = tile[0:8]
+            for v in range(1, 16):
+                row = jnp.where((lane >> 3) == v, tile[8 * v : 8 * v + 8], row)
+            lam_ref[t * GROUPS + g] = jnp.sum(jnp.where(corner, row, 0.0), axis=0, keepdims=True)
         return carry
 
     lax.fori_loop(0, TASKS, finish, 0)
+    for plane in range(NZ):
+        put(plane).wait()
 
 
 def attend_prompts(order, counts, spans, q_all, keys, values):
@@ -316,28 +383,33 @@
     return pl.pallas_call(
         prompt_kernel,
         out_shape=(
-            jax.ShapeDtypeStruct((rows, HD), BF16),
+            jax.ShapeDtypeStruct((TASKS, SHARD, HD), BF16),
             jax.ShapeDtypeStruct((TASKS * GROUPS, 1, 128), F32),
         ),
         in_specs=[SMEM_SPEC] * 3 + [VMEM_SPEC] * 3,
-        out_specs=(VMEM_SPEC, VMEM_SPEC),
+        out_specs=(HBM_SPEC, VMEM_SPEC),
         scratch_shapes=[
             pltpu.VMEM((rows, 128), F32),
             pltpu.VMEM((rows, 128), F32),
             pltpu.VMEM((ROWS, 128), F32),
             pltpu.VMEM((ROWS, 256), F32),
             pltpu.VMEM((ROWS, 128), F32),
+            pltpu.VMEM((TASKS, SHARD, HD), BF16),
             pltpu.SMEM((16 * SLOTS,), jnp.int32),
             pltpu.SMEM((16,), jnp.int32),
+            pltpu.SemaphoreType.DMA((NZ,)),
         ],
-        compiler_params=pltpu.CompilerParams(vmem_limit_bytes=56 * 2**20),
+        compiler_params=pltpu.CompilerParams(vmem_limit_bytes=62 * 2**20),
+        cost_estimate=pl.CostEstimate(
+            flops=2 * 10**10, bytes_accessed=2 * 10**7, transcendentals=10**7
+        ),
         name="attend_prompts",
     )(order, counts, spans, q_all.reshape(rows, HD), keys, values)
 
 
 def merge_kernel(
-    part_in, lam_in, own_ref, own_lam_ref, w_ref, out_ref,
-    part_ref, lam_ref, land_ref, lland_ref, mix_ref, a_ref, p_ref, c_ref, y_ref, yland_ref, r_ref,
+    part_in, lam_in, own_ref, own_lam_ref, w0_ref, w1_ref, w2_ref, w3_ref, out_ref,
+    part_ref, lam_ref, land_ref, lland_ref, mix_ref, a_ref, p_ref, c_ref, y_ref, yland_ref, mine_ref, r_ref,
     in_sem, send_sems, recv_sems, lsend_sems, lrecv_sems,
     a_sems, c_sems, y_sems, x_sems,
 ):
@@ -345,16 +417,20 @@
     tp = lax.axis_index("tp")
     y, core = tp // 2, lax.rem(tp, 2)
     partner = {"tp": 2 * y + 1 - core}
-    up, down = ({"tp": 2 * lax.rem(y + d, 4) + core} for d in (1, 3))
-    load = pltpu.make_async_copy(part_in, part_ref, in_sem.at[0])
-    lload = pltpu.make_async_copy(lam_in, lam_ref, in_sem.at[1])
-    load.start()
+    loads = {}
+    for dz in (4, 3, -3, 2, -2, 1, -1, 0):
+        plane = pl.ds(task_at(z - dz, 0), NX)
+        loads[dz] = pltpu.make_async_copy(
+            part_in.at[plane], part_ref.at[plane], in_sem.at[dz + 3]
+        )
+        loads[dz].start()
+    lload = pltpu.make_async_copy(lam_in, lam_ref, in_sem.at[8])
     lload.start()
-    greet(plane_neighbours(z, x) + [{"task": task_at(z, x + 2)}, partner, up, down])
-    load.wait()
+    greet(plane_neighbours(z, x) + [{"task": task_at(z, x + 2)}, partner]
+          + [{"tp": 2 * lax.rem(y + d, 4) + core} for d in (1, 2, 3)])
     lload.wait()
     offsets, at = {}, 0
-    for hop in TREE:
+    for hop in BACK:
         offsets[hop.index] = at
         at += hop.high - hop.low
 
@@ -415,13 +491,17 @@
                 lam_ref[origin * GROUPS + g] = top + jnp.log(total)
                 part_ref[origin, pl.ds(128 * g, 128), :] = mixed.astype(BF16)
 
-    for hop in reversed(TREE):
+    for hop in reversed(BACK):
+        if hop.dz in loads:
+            loads.pop(hop.dz).wait()
         if hop.kids:
             merge(task_at(z - hop.dz, x - hop.dx), hop.low, hop.high, hop.kids, False)
         for copy in copies(hop):
             copy.start()
-    merge(task_at(z, x), 0, SHARD, [hop for hop in TREE if not hop.deps], True)
-    for hop in TREE:
+    for load in loads.values():
+        load.wait()
+    merge(task_at(z, x), 0, SHARD, [hop for hop in BACK if not hop.deps], True)
+    for hop in BACK:
         for copy in copies(hop):
             copy.wait_send()
 
@@ -465,8 +545,8 @@
     def project(offsets):
         first = slot_of[offsets[0]]
         rows = a_ref[pl.ds(96 * first, 96 * len(offsets)), :]
-        for q in range(NX):
-            product = jnp.dot(rows, w_ref[q], preferred_element_type=F32)
+        for q, w_ref in enumerate((w0_ref, w1_ref, w2_ref, w3_ref)):
+            product = jnp.dot(rows, w_ref[...], preferred_element_type=F32)
             for i, offset in enumerate(offsets):
                 p_ref[block_of(offset), :, pl.ds(256 * q, 256)] = product[96 * i : 96 * i + 96]
         for offset in offsets:
@@ -476,6 +556,14 @@
             def _():
                 copy.start()
 
+    def hand_on(offset):
+        block = block_of(offset)
+        way = lax.rem(block // 2 - y + 4, 4)
+        index = jnp.maximum(way - 1, 0)
+        return way > 0, remote(
+            y_ref.at[slot_of[offset]], yland_ref.at[index], y_sems, index, {"tp": block}
+        )
+
     def take_over(offsets):
         for offset in offsets:
             away, copy = hand_over(offset)
@@ -483,8 +571,18 @@
             @pl.when(jnp.logical_not(away))
             def _():
                 copy.wait_recv()
-                block = block_of(offset)
-                p_ref[block] = p_ref[block] + c_ref[slot_of[offset]]
+                slot = slot_of[offset]
+                total = p_ref[block_of(offset)] + c_ref[slot]
+                onward, share = hand_on(offset)
+
+                @pl.when(onward)
+                def _():
+                    y_ref[slot] = total.astype(BF16)
+                    share.start()
+
+                @pl.when(jnp.logical_not(onward))
+                def _():
+                    mine_ref[...] = total
 
     for hop in hops:
         if hop[1] == 1:
@@ -502,46 +600,26 @@
             take_over(turns[step - 1])
     take_over(turns[-1])
 
-    def tp_block(d):
-        return 2 * lax.rem(y + d, 4) + core
-
-    top, low = pl.ds(0, 48), pl.ds(48, 48)
-    far, plus, minus = tp_block(2), tp_block(1), tp_block(3)
-    y_ref[0] = p_ref[far].astype(BF16)
-    y_ref[1, low] = p_ref[plus, pl.ds(48, 48), :].astype(BF16)
-    y_ref[2, top] = p_ref[minus, pl.ds(0, 48), :].astype(BF16)
-    relay_up = remote(y_ref.at[0, top], yland_ref.at[0, top], y_sems, 0, up)
-    relay_down = remote(y_ref.at[0, low], yland_ref.at[0, low], y_sems, 1, down)
-    early_up = remote(y_ref.at[1, low], yland_ref.at[1, low], y_sems, 2, up)
-    early_down = remote(y_ref.at[2, top], yland_ref.at[2, top], y_sems, 3, down)
-    late_up = remote(y_ref.at[1, top], yland_ref.at[1, top], y_sems, 4, up)
-    late_down = remote(y_ref.at[2, low], yland_ref.at[2, low], y_sems, 5, down)
-    for copy in (relay_up, relay_down, early_up, early_down):
-        copy.start()
-    relay_up.wait_recv()
-    y_ref[1, top] = (p_ref[plus, pl.ds(0, 48), :] + yland_ref[0, top].astype(F32)).astype(BF16)
-    late_up.start()
-    relay_down.wait_recv()
-    y_ref[2, low] = (p_ref[minus, pl.ds(48, 48), :] + yland_ref[0, low].astype(F32)).astype(BF16)
-    late_down.start()
-    for copy in (early_up, early_down, late_up, late_down):
-        copy.wait_recv()
-    mine = p_ref[tp_block(0)] + yland_ref[1].astype(F32) + yland_ref[2].astype(F32)
+    for way in range(3):
+        remote(y_ref.at[0], yland_ref.at[way], y_sems, way, partner).wait_recv()
+    mine = mine_ref[...]
+    for way in range(3):
+        mine = mine + yland_ref[way].astype(F32)
     for q in range(NX):
-        r_ref[q] = mine[:, 256 * q : 256 * q + 256]
+        r_ref[q] = mine[:, 256 * q : 256 * q + 256].astype(BF16)
 
     shares = []
     for d in (1, 2, 3):
         peer = lax.rem(x + d, NX)
         share = remote(
-            r_ref.at[peer], out_ref.at[x], x_sems, d - 1, {"task": task_at(z, peer)}
+            r_ref.at[d], out_ref.at[x], x_sems, d - 1, {"task": task_at(z, peer)}
         )
         share.start()
         shares.append(share)
-    out_ref[x] = r_ref[x]
+    out_ref[x] = r_ref[0]
     for share in shares:
         share.wait_recv()
-    for share in shares + [relay_up, relay_down, early_up, early_down, late_up, late_down]:
+    for share in shares:
         share.wait_send()
     for hop in hops:
         row_copy(*hop).wait_send()
@@ -553,14 +631,20 @@
             def _():
                 copy.wait_send()
 
+            onward, share = hand_on(offset)
+
+            @pl.when(jnp.logical_not(away) & onward)
+            def _():
+                share.wait_send()
+
 
 def merge_parts(parts, lams, own, own_lam, weights):
-    hops = len(TREE)
-    landed = sum(hop.high - hop.low for hop in TREE)
+    hops = len(BACK)
+    landed = sum(hop.high - hop.low for hop in BACK)
     return pl.pallas_call(
         merge_kernel,
-        out_shape=jax.ShapeDtypeStruct((NX, 96, 256), F32),
-        in_specs=[ANY_SPEC, ANY_SPEC, VMEM_SPEC, VMEM_SPEC, VMEM_SPEC],
+        out_shape=jax.ShapeDtypeStruct((NX, 96, 256), BF16),
+        in_specs=[HBM_SPEC, ANY_SPEC] + [VMEM_SPEC] * 6,
         out_specs=VMEM_SPEC,
         scratch_shapes=[
             pltpu.VMEM((TASKS, SHARD, HD), BF16),
@@ -571,24 +655,25 @@
             pltpu.VMEM((8 * 96, 1024), BF16),
             pltpu.VMEM((8, 96, 1024), F32),
             pltpu.VMEM((8, 96, 1024), F32),
+            pltpu.VMEM((8, 96, 1024), BF16),
             pltpu.VMEM((3, 96, 1024), BF16),
-            pltpu.VMEM((3, 96, 1024), BF16),
-            pltpu.VMEM((NX, 96, 256), F32),
-            pltpu.SemaphoreType.DMA((2,)),
+            pltpu.VMEM((96, 1024), F32),
+            pltpu.VMEM((NX, 96, 256), BF16),
+            pltpu.SemaphoreType.DMA((9,)),
             pltpu.SemaphoreType.DMA((hops,)),
             pltpu.SemaphoreType.DMA((hops,)),
             pltpu.SemaphoreType.DMA((hops,)),
             pltpu.SemaphoreType.DMA((hops,)),
             pltpu.SemaphoreType.DMA((2, 16)),
             pltpu.SemaphoreType.DMA((2, 8)),
-            pltpu.SemaphoreType.DMA((2, 6)),
+            pltpu.SemaphoreType.DMA((2, 3)),
             pltpu.SemaphoreType.DMA((2, 3)),
         ],
         compiler_params=pltpu.CompilerParams(
-            collective_id=1, has_side_effects=True, vmem_limit_bytes=56 * 2**20
+            collective_id=1, has_side_effects=True, vmem_limit_bytes=62 * 2**20
         ),
         name="merge_parts",
-    )(parts.reshape(TASKS, SHARD, HD), lams, own, own_lam, weights)
+    )(parts, lams, own, own_lam, *weights)
 
 
 def on_device(
@@ -603,10 +688,13 @@
         q, suffix_keys, suffix_values, new_keys, new_values, decoded_lens
     )
     weight, q_all = lax.optimization_barrier((out_weight, q_all))
-    rings = [[NX * z + x for x in range(NX)] for z in range(NZ)]
-    weights = lax.all_gather(weight, "task", axis_index_groups=rings)
+    weights = [weight]
+    for d in (1, 2, 3):
+        pairs = [(NX * z + (x + d) % NX, NX * z + x) for z in range(NZ) for x in range(NX)]
+        weights.append(lax.ppermute(weight, "task", pairs))
     parts, lams = attend_prompts(order, share_counts, span_perm, q_all, prompt_keys, prompt_values)
-    return merge_parts(parts, lams, own, own_lam, weights).reshape(NX * 96, 256)
+    out = merge_parts(parts, lams, own, own_lam, weights)
+    return out.reshape(NX * 96, 256).astype(F32)
 
 
 def solution(mesh):

time: 220 us -> 183 us (0.83); the launches traced: 218 us -> 184 us
  Pallas kernels: 194 us -> 174 us
  between operations: 13.4 us -> 0.08 us
  local copies, waits for them, and re-layouts: 9.43 us -> 2.73 us
  starting transfers between devices: 0.01 us -> 3.73 us
    pallas_call x1, Pallas kernels: 51.7 us -> 26.6 us  [attend_prompts(): pl.pallas_call(prompt_kernel, out_shape=(jax.ShapeDtypeStruct((TASKS, SHA...]
    unnamed x17 -> x8, local copies, waits for them, and re-layouts: 8.41 us -> 0.98 us
    ppermute x0 -> x3, starting transfers between devices: none -> 3.73 us  [on_device(): weights.append(lax.ppermute(weight, 'task', pairs))]
    pallas_call x1, Pallas kernels: 44.7 us -> 47.6 us  [gather_queries(): pl.pallas_call(gather_kernel, out_shape=(jax.ShapeDtypeStruct((TASKS, SHA...]
    pallas_call x1, Pallas kernels: 97.7 us -> 100 us  [merge_parts(): pl.pallas_call(merge_kernel, out_shape=jax.ShapeDtypeStruct((NX, 96, 256)...]
  transfers between devices with their start and end apart: 1 -> 3, of which waited for: 0 -> 0; matrix products, arithmetic and copies ran while one was open for 1% -> 1% of each run, Pallas kernels for 24% -> 14%
where the time goes in v3:
time: 183 us; the launch traced here: 184 us
  Pallas kernels  174 us (95%)
  starting transfers between devices  3.73 us (2%)
  other arithmetic  2.79 us (2%)
  local copies, waits for them, and re-layouts  2.73 us (1%)
    pallas_call x1, Pallas kernels, merge_parts(): pl.pallas_call(merge_kernel, out_shape=jax.ShapeDtypeStruct((NX, 96, 256)...  100 us
    pallas_call x1, Pallas kernels, gather_queries(): pl.pallas_call(gather_kernel, out_shape=(jax.ShapeDtypeStruct((TASKS, SHA...  47.6 us
    pallas_call x1, Pallas kernels, attend_prompts(): pl.pallas_call(prompt_kernel, out_shape=(jax.ShapeDtypeStruct((TASKS, SHA...  26.6 us
    ppermute x3, starting transfers between devices, on_device(): weights.append(lax.ppermute(weight, 'task', pairs))  3.73 us
  transfers between devices with their start and end apart: 3, of which 0 were waited for; matrix products, arithmetic and copies ran while one was open for 1% of the time, Pallas kernels for 14%

profile of v3, /device:TPU:49, one launch (start us, length us, event | category | flops | bytes accessed | tf_op | source)
XLA Modules:
  0.0 183.6 jit_solution(6893240160185861948)
XLA Ops:
  0.0 0.0 copy-start
  0.0 0.0 copy-start.3
  0.0 1.7 reshape.10.q_ref
  1.8 47.6 %gather_queries.1 = (bf16[32,768,128]{2,1,0:T(8,128)(2,1)}, f32[768,128]{1,0:T(8,128)}, f32[6,1,128]{2,1,0:T(1,128)}) custom-call(bf16[768,128]{1,0:T(8,128)(2,1)} %reshape.10.q_ref, bf16[8192,128]{1,0:T(8,128)(2,1)} %sk_ref.1, bf16[8192,128]{1,0:T(8,128)(2,1)} %sv_ref.1, bf16[96,128]{1,0:T(8,128)(2,1)} %nk_ref.1, bf16[96,128]{1,0:T(8,128)(2,1)} %nv_ref.1, ...), custom_call_target="tpu_custom_call" | custom-call | tf_op jit(solution)/shard_map/gather_queries/pallas_call | solution.py:210
  49.4 0.0 copy-done
  49.4 0.9 collective-permute-start.2
  50.3 2.1 %collective-permute-start.1 = (bf16[1024,256]{1,0:T(8,128)(2,1)S(1)}, bf16[1024,256]{1,0:T(8,128)(2,1)S(1)}, u32[]{:S(2)}, u32[]{:S(2)}) collective-permute-start(bf16[1024,256]{1,0:T(8,128)(2,1)S(1)} %copy-done), channel_id=1, source_target_pairs={{16,0},{24,8},{0,16},{8,24},{48,32},{56,40},{32,48},{40,56},{80,64... | collective-permute-start | bytes 1572872 | tf_op jit(solution)/shard_map/ppermute | solution.py:694
  52.4 0.7 collective-permute-start
  53.1 0.0 copy-done.3
  53.1 1.1 select_reduce_fusion.order_ref
  54.2 26.6 %attend_prompts.1 = (bf16[32,768,128]{2,1,0:T(8,128)(2,1)}, f32[192,1,128]{2,1,0:T(1,128)}) custom-call(s32[1024]{0:T(1024)} %select_reduce_fusion.order_ref, s32[16]{0:T(128)} %counts_ref.1, s32[16]{0:T(128)} %span_ref.1, bf16[24576,128]{1,0:T(8,128)(2,1)} %bitcast.4, bf16[4096,128]{1,0:T(8,128)(2,1)} %k_ref.1, bf16[4096,128]{1,0:T(8,128)(2,1)} %v_ref.1), custom_call_target="tpu_custom_call" | custom-call | flops 20000000000 | bytes 20000000 | tf_op jit(solution)/shard_map/attend_prompts/pallas_call | solution.py:383
  80.8 0.0 collective-permute-done.2.w3_ref
  80.8 0.0 copy-start.1
  80.8 0.0 collective-permute-done.1.w2_ref
  80.8 0.0 copy-start.2
  80.8 0.0 collective-permute-done.w1_ref
  80.8 0.8 copy-done.1
  81.6 0.2 copy-done.2
  81.8 100.1 %merge_parts.1 = bf16[4,96,256]{2,1,0:T(8,128)(2,1)} custom-call(bf16[32,768,128]{2,1,0:T(8,128)(2,1)} %get-tuple-element.14.part_in, f32[192,1,128]{2,1,0:T(1,128)} %get-tuple-element.15.lam_in, f32[768,128]{1,0:T(8,128)} %get-tuple-element.16.own_ref, f32[6,1,128]{2,1,0:T(1,128)} %get-tuple-element.17.own_lam_ref, bf16[1024,256]{1,0:T(8,128)(2,1)} %w0_ref, ...), custom_call_target="tpu_custom_call" | custom-call | tf_op jit(solution)/shard_map/merge_parts/pallas_call | solution.py:644
  181.9 1.7 bitcast_convert_fusion
Async XLA Ops:
  0.0 49.4 %copy-start = (bf16[1024,256]{1,0:T(8,128)(2,1)S(1)}, bf16[1024,256]{1,0:T(8,128)(2,1)}, u32[]{:S(2)}) copy-start(bf16[1024,256]{1,0:T(8,128)(2,1)} %w0_ref) | copy-start | bytes 1572868
  0.0 53.1 %copy-start.3 = (s32[1024]{0:T(1024)S(1)}, s32[1024]{0:T(1024)}, u32[]{:S(2)}) copy-start(s32[1024]{0:T(1024)} %param.22) | copy-start | bytes 12292
  49.4 31.4 %collective-permute-start.2 = (bf16[1024,256]{1,0:T(8,128)(2,1)S(1)}, bf16[1024,256]{1,0:T(8,128)(2,1)S(1)}, u32[]{:S(2)}, u32[]{:S(2)}) collective-permute-start(bf16[1024,256]{1,0:T(8,128)(2,1)S(1)} %copy-done), channel_id=1, source_target_pairs={{24,0},{0,8},{8,16},{16,24},{56,32},{32,40},{40,48},{48,56},{88,64... | collective-permute-start | bytes 1572872 | tf_op jit(solution)/shard_map/ppermute | solution.py:694
  50.3 30.5 %collective-permute-start.1 = (bf16[1024,256]{1,0:T(8,128)(2,1)S(1)}, bf16[1024,256]{1,0:T(8,128)(2,1)S(1)}, u32[]{:S(2)}, u32[]{:S(2)}) collective-permute-start(bf16[1024,256]{1,0:T(8,128)(2,1)S(1)} %copy-done), channel_id=1, source_target_pairs={{16,0},{24,8},{0,16},{8,24},{48,32},{56,40},{32,48},{40,56},{80,64... | collective-permute-start | bytes 1572872 | tf_op jit(solution)/shard_map/ppermute | solution.py:694
  52.4 28.4 %collective-permute-start = (bf16[1024,256]{1,0:T(8,128)(2,1)S(1)}, bf16[1024,256]{1,0:T(8,128)(2,1)}, u32[]{:S(2)}, u32[]{:S(2)}) collective-permute-start(bf16[1024,256]{1,0:T(8,128)(2,1)S(1)} %copy-done), channel_id=1, source_target_pairs={{8,0},{16,8},{24,16},{0,24},{40,32},{48,40},{56,48},{32,56},{72,64... | collective-permute-start | bytes 1572872 | tf_op jit(solution)/shard_map/ppermute | solution.py:694
  80.8 0.8 copy-start.1
  80.8 1.0 copy-start.2
